TPU v7x, 32 devices: a whole 2x2x4 slice. The times are simulated.
32 devices in a mesh: cast: 4 (over x, core), span: 8 (over z, y).
Axes of the slice: x: 2, y: 2, z: 4, core: 2. Of those that a mesh axis runs over, the one named last changes fastest.
Arguments:
- phase: int32 [16, 64, 1024], P(None, 'cast', 'span'), may hold values from 0 to 2
- viscosity_table: float32 [3], replicated, may hold values from 0.25 to 4
- pressure_source: float32 [16, 64, 1024], P(None, 'cast', 'span'), may hold values from -6 to 6
Outputs:
- solution_field: float32 [16, 64, 1024], P(None, 'cast', 'span')
- residual: float32 [16, 64, 1024], P(None, 'cast', 'span')
All inputs are finite; a program needn't handle non-finite values.
Results may differ from a plain program's by a relative error of at most 0.0003.
Values sent between devices are 32-bit elements; how exact they have to be, the bound alone decides.
A program may use at most 64 MiB of HBM per device.

v0:
```python
import jax
import jax.numpy as jnp
from jax import lax
from jax.sharding import PartitionSpec as P

LEVELS = 3
PRE = 2
POST = 2
COARSE = 8


relax_weight = 0.8


def padded(shard, sides, width):
    for axis, dim in sides:
        size, length = (lax.axis_size(axis), shard.shape[dim])
        up = [(i, (i + 1) % size) for i in range(size - 1)]
        down = [(j, i) for i, j in up]
        last = lax.slice_in_dim(shard, length - width, length, axis=dim)
        initial = lax.slice_in_dim(shard, 0, width, axis=dim)
        before = lax.ppermute(last, axis, up)
        after = lax.ppermute(initial, axis, down)
        shard = jnp.concatenate([before, shard, after], axis=dim)
    return shard


def passed_along(value, axis, steps):
    count = lax.axis_size(axis)
    pairs = [(source, (source + steps) % count) for source in range(count)]
    return lax.ppermute(value, axis, pairs)


def from_partner(shard, axis, bit):
    return lax.ppermute(shard, axis, [(i, i ^ 1 << bit) for i in range(lax.axis_size(axis))])


def harmonic(lower, upper):
    return 2.0 * lower * upper / (lower + upper)


def coarsen(values):
    height, length, width = values.shape
    return jnp.mean(values.reshape(height // 2, 2, length // 2, 2, width // 2, 2), axis=(1, 3, 5))


def refine(values):
    return jnp.repeat(jnp.repeat(jnp.repeat(values, 2, axis=0), 2, axis=1), 2, axis=2)


def extend(values, margin, stride, edge_copy):
    grown = padded(values, (("cast", 1),), margin)
    if edge_copy:
        where_cast = lax.axis_index("cast")
        first_rows = grown[:, margin : margin + 1]
        last_rows = grown[:, -margin - 1 : -margin]
        lower_part = jnp.where(where_cast == 0, first_rows, grown[:, :margin])
        upper_part = jnp.where(
            where_cast == lax.axis_size("cast") - 1, last_rows, grown[:, -margin:]
        )
        grown = jnp.concatenate([lower_part, grown[:, margin:-margin], upper_part], axis=1)
    if stride % lax.axis_size("span") == 0:
        before = grown[:, :, -margin:]
        after = grown[:, :, :margin]
    else:
        before = passed_along(grown[:, :, -margin:], "span", stride)
        after = passed_along(grown[:, :, :margin], "span", -stride)
    return jnp.concatenate([before, grown, after], axis=2)


def prepare(coeff, margin, stride):
    spread_coeff = extend(coeff, margin, stride, True)
    cast_faces = harmonic(spread_coeff[:, :-1], spread_coeff[:, 1:])
    span_faces = harmonic(spread_coeff[:, :, :-1], spread_coeff[:, :, 1:])
    inner = spread_coeff[:, 1:-1, 1:-1]
    cast_lower = cast_faces[:, :-1, 1:-1]
    cast_upper = cast_faces[:, 1:, 1:-1]
    span_lower = span_faces[:, 1:-1, :-1]
    span_upper = span_faces[:, 1:-1, 1:]
    height_inner = harmonic(inner[:-1], inner[1:])
    flat = jnp.zeros_like(inner[:1])
    height_lower = jnp.concatenate([flat, height_inner], axis=0)
    height_upper = jnp.concatenate([height_inner, flat], axis=0)
    diagonal = cast_lower + cast_upper + span_lower + span_upper + height_lower + height_upper
    return (cast_lower, cast_upper, span_lower, span_upper, height_lower, height_upper, diagonal)


def stencil(grown, faces, scale):
    cast_lower, cast_upper, span_lower, span_upper, height_lower, height_upper, diagonal = [
        face for face in faces
    ]
    center = grown[:, 1:-1, 1:-1]
    flat = jnp.zeros_like(center[:1])
    below = jnp.concatenate([flat, center[:-1]], axis=0)
    above = jnp.concatenate([center[1:], flat], axis=0)
    near = (
        cast_lower * grown[:, :-2, 1:-1]
        + cast_upper * grown[:, 2:, 1:-1]
        + span_lower * grown[:, 1:-1, :-2]
        + span_upper * grown[:, 1:-1, 2:]
        + height_lower * below
        + height_upper * above
    )
    return (center, diagonal, scale * (diagonal * center - near))


def smooth(source, source_wide, faces, margin, stride, scale, sweeps, start):
    if start is None:
        values = relax_weight * source / (scale * faces[6])
        remaining = sweeps - 1
    else:
        values = start
        remaining = sweeps
    while remaining > 0:
        number = min(margin, remaining)
        grown = extend(values, number, stride, False)
        center, diagonal, image = stencil(grown, faces, scale)
        grown = center + relax_weight * (source_wide - image) / (scale * diagonal)
        values = grown
        remaining = remaining - number
    return values


def shards(phase, viscosity_table, pressure_source):
    margin = 1
    viscosity = jnp.where(
        phase == 0,
        viscosity_table[0],
        jnp.where(phase == 1, viscosity_table[1], viscosity_table[2]),
    )
    coeff = 1.0 / viscosity
    source = pressure_source
    stored = []
    for level in range(LEVELS):
        stride = 2**level
        scale = 0.25**level
        faces = prepare(coeff, margin, stride)
        source_wide = source
        values = smooth(source, source_wide, faces, margin, stride, scale, PRE, None)
        center, diagonal, image = stencil(extend(values, 1, stride, False), faces, scale)
        remainder = source - image
        stored.append((values, faces, source, source_wide, stride, scale))
        stacked = jnp.stack([coarsen(coeff), coarsen(remainder)])
        partner = from_partner(stacked, "span", level)
        upper_half = jnp.right_shift(lax.axis_index("span"), level) & 1 == 1
        stacked = jnp.where(
            upper_half,
            jnp.concatenate([partner, stacked], axis=3),
            jnp.concatenate([stacked, partner], axis=3),
        )
        coeff = stacked[0]
        source = stacked[1]
    stride = 2**LEVELS
    scale = 0.25**LEVELS
    faces = prepare(coeff, margin, stride)
    source_wide = source
    values = smooth(source, source_wide, faces, margin, stride, scale, COARSE, None)
    for level in reversed(range(LEVELS)):
        kept, faces, source, source_wide, stride, scale = stored[level]
        half_width = values.shape[2] // 2
        upper_bit = jnp.right_shift(lax.axis_index("span"), level) & 1
        values = lax.dynamic_slice_in_dim(values, upper_bit * half_width, half_width, 2)
        values = kept + refine(values)
        values = smooth(source, source_wide, faces, margin, stride, scale, POST, values)
    finest_faces = stored[0][1]
    center, diagonal, image = stencil(extend(values, 1, 1, False), finest_faces, 1.0)
    residual = pressure_source - image
    return (values, residual)


def solution(mesh):
    placed = (P(None, "cast", "span"), P(), P(None, "cast", "span"))
    return jax.shard_map(
        shards,
        mesh=mesh,
        in_specs=placed,
        out_specs=(P(None, "cast", "span"), P(None, "cast", "span")),
        check_vma=False,
    )
```

profile of v0, /device:TPU:0, one launch (start us, length us, event | category | flops | bytes accessed | tf_op | source)
XLA Modules:
  0.0 350.0 jit_solution(13801896614650900390)
XLA Ops:
  2.1 2.8 select_divide_fusion
  4.9 2.4 collective-permute-start
  8.7 3.8 %collective-permute-done.1 = f32[16,1,128]{2,0,1:T(8,128)S(1)} collective-permute-done((f32[16,1,128]{2,0,1:T(8,128)S(1)}, f32[16,1,128]{2,0,1:T(8,128)S(1)}, u32[]{:S(2)}, u32[]{:S(2)}) %collective-permute-start.1) | collective-permute-done | bytes 8224 | tf_op jit(solution)/shard_map/ppermute | solution.py:23
  14.2 3.2 collective-permute-start.3
  17.4 3.2 collective-permute-done.2
  25.1 2.9 collective-permute-start.4
  31.3 4.7 %collective-permute-start.7 = (f32[16,18,1]{2,0,1:T(8,128)S(1)}, f32[16,18,1]{2,0,1:T(8,128)S(1)}, u32[]{:S(2)}, u32[]{:S(2)}) collective-permute-start(f32[16,18,1]{2,0,1:T(8,128)S(1)} %get-tuple-element.41), channel_id=1, source_target_pairs={{0,7},{1,0},{2,1},{3,2},{4,3},{5,4},{6,5},{7,6},{8,15},{9,8},{10,9... | collective-permute-start | bytes 3464 | tf_op jit(solution)/shard_map/ppermute | solution.py:31
  36.0 3.8 %collective-permute-done.6 = f32[16,18,1]{2,0,1:T(8,128)S(1)} collective-permute-done((f32[16,18,1]{2,0,1:T(8,128)S(1)}, f32[16,18,1]{2,0,1:T(8,128)S(1)}, u32[]{:S(2)}, u32[]{:S(2)}) %collective-permute-start.6) | collective-permute-done | bytes 1184 | tf_op jit(solution)/shard_map/ppermute | solution.py:31
  41.3 2.7 collective-permute-start.8
  43.9 9.7 %reshape.151 = f32[8,2,8,2,64,2]{5,4,3,2,1,0:T(8,128)} reshape(f32[16,16,128]{2,1,0:T(8,128)S(1)} %select_divide_fusion) | data formatting | bytes 262144 | tf_op jit(solution)/shard_map/reshape | solution.py:44
  53.7 4.1 %reduce_sum.54 = f32[8,8,64]{2,1,0:T(8,128)S(1)} reduce(f32[8,2,8,2,64,2]{5,4,3,2,1,0:T(8,128)} %reshape.151, f32[]{:T(128)} %constant.23.clone.1), dimensions={1,3,5}, to_apply=%region_0.1 | reduce | flops 28672 | bytes 147460 | tf_op jit(solution)/shard_map/reduce_sum | solution.py:44
  60.9 4.7 %collective-permute-start.11 = (f32[16,18,1]{2,0,1:T(8,128)S(1)}, f32[16,18,1]{2,0,1:T(8,128)S(1)}, u32[]{:S(2)}, u32[]{:S(2)}) collective-permute-start(f32[16,18,1]{2,0,1:T(8,128)S(1)} %get-tuple-element.37), channel_id=1, source_target_pairs={{0,7},{1,0},{2,1},{3,2},{4,3},{5,4},{6,5},{7,6},{8,15},{9,8},{10,9... | collective-permute-start | bytes 3464 | tf_op jit(solution)/shard_map/ppermute | solution.py:31
  65.7 3.8 %collective-permute-done.10 = f32[16,18,1]{2,0,1:T(8,128)S(1)} collective-permute-done((f32[16,18,1]{2,0,1:T(8,128)S(1)}, f32[16,18,1]{2,0,1:T(8,128)S(1)}, u32[]{:S(2)}, u32[]{:S(2)}) %collective-permute-start.10) | collective-permute-done | bytes 1184 | tf_op jit(solution)/shard_map/ppermute | solution.py:31
  71.4 9.7 %reshape.152 = f32[8,2,8,2,64,2]{5,4,3,2,1,0:T(8,128)} reshape(f32[16,16,128]{2,1,0:T(8,128)S(1)} %fusion.43) | data formatting | bytes 262144 | tf_op jit(solution)/shard_map/reshape | solution.py:44
  81.1 4.1 %reduce_sum.55 = f32[8,8,64]{2,1,0:T(8,128)S(1)} reduce(f32[8,2,8,2,64,2]{5,4,3,2,1,0:T(8,128)} %reshape.152, f32[]{:T(128)} %constant.23.clone.1), dimensions={1,3,5}, to_apply=%region_1.2 | reduce | flops 28672 | bytes 147460 | tf_op jit(solution)/shard_map/reduce_sum | solution.py:44
  85.4 4.7 %collective-permute-done.12 = f32[2,8,8,64]{3,2,1,0:T(8,128)S(1)} collective-permute-done((f32[2,8,8,64]{3,2,1,0:T(8,128)S(1)}, f32[2,8,8,64]{3,2,1,0:T(8,128)S(1)}, u32[]{:S(2)}, u32[]{:S(2)}) %collective-permute-start.12) | collective-permute-done | bytes 32800 | tf_op jit(solution)/shard_map/ppermute | solution.py:35
  97.1 2.5 collective-permute-start.16
  102.9 2.9 collective-permute-start.17
  107.2 2.8 reshape_squeeze.6
  111.7 3.2 collective-permute-start.20
  118.1 2.4 collective-permute-start.21
  121.8 3.8 %collective-permute-done.22 = f32[8,1,128]{2,1,0:T(1,128)S(1)} collective-permute-done((f32[8,1,128]{2,1,0:T(1,128)S(1)}, f32[8,1,128]{2,1,0:T(1,128)S(1)}, u32[]{:S(2)}, u32[]{:S(2)}) %collective-permute-start.22) | collective-permute-done | bytes 4128 | tf_op jit(solution)/shard_map/ppermute | solution.py:23
  126.8 3.0 collective-permute-start.24
  133.2 2.8 reshape.153
  137.7 2.4 collective-permute-done.25
  140.3 2.4 collective-permute-start.26
  144.7 2.5 collective-permute-done.27
  147.3 2.6 collective-permute-start.28
  151.9 2.6 collective-permute-done.29
  154.8 2.8 collective-permute-start.30
  159.0 2.7 collective-permute-done.31
  162.1 2.6 collective-permute-start.33
  166.9 3.2 collective-permute-start.34
  173.8 2.6 collective-permute-start.36
  178.4 2.6 collective-permute-done.37
  182.2 4.2 %collective-permute-done.38 = f32[2,2,2,64]{3,2,1,0:T(2,128)S(1)} collective-permute-done((f32[2,2,2,64]{3,2,1,0:T(2,128)S(1)}, f32[2,2,2,64]{3,2,1,0:T(2,128)S(1)}, u32[]{:S(2)}, u32[]{:S(2)}) %collective-permute-start.38) | collective-permute-done | bytes 2080 | tf_op jit(solution)/shard_map/ppermute | solution.py:35
  189.5 3.8 %collective-permute-done.40 = f32[2,1,128]{2,1,0:T(1,128)S(1)} collective-permute-done((f32[2,1,128]{2,1,0:T(1,128)S(1)}, f32[2,1,128]{2,1,0:T(1,128)S(1)}, u32[]{:S(2)}, u32[]{:S(2)}) %collective-permute-start.40) | collective-permute-done | bytes 1056 | tf_op jit(solution)/shard_map/ppermute | solution.py:23
  193.7 4.3 %collective-permute-start.41 = (f32[2,1,128]{2,1,0:T(1,128)S(1)}, f32[2,1,128]{2,1,0:T(1,128)S(1)}, u32[]{:S(2)}, u32[]{:S(2)}) collective-permute-start(f32[2,1,128]{2,1,0:T(1,128)S(1)} %get-tuple-element.205), channel_id=1, source_target_pairs={{0,8},{8,16},{16,24},{1,9},{9,17},{17,25},{2,10},{10,18},{18,26},{... | collective-permute-start | bytes 3080 | tf_op jit(solution)/shard_map/ppermute | solution.py:22
  201.2 3.8 %collective-permute-start.43 = (f32[2,1,128]{2,1,0:T(1,128)S(1)}, f32[2,1,128]{2,1,0:T(1,128)S(1)}, u32[]{:S(2)}, u32[]{:S(2)}) collective-permute-start(f32[2,1,128]{2,1,0:T(1,128)S(1)} %get-tuple-element.201), channel_id=1, source_target_pairs={{0,8},{8,16},{16,24},{1,9},{9,17},{17,25},{2,10},{10,18},{18,26},{... | collective-permute-start | bytes 3080 | tf_op jit(solution)/shard_map/ppermute | solution.py:22
  208.3 3.8 %collective-permute-start.45 = (f32[2,1,128]{2,1,0:T(1,128)S(1)}, f32[2,1,128]{2,1,0:T(1,128)S(1)}, u32[]{:S(2)}, u32[]{:S(2)}) collective-permute-start(f32[2,1,128]{2,1,0:T(1,128)S(1)} %get-tuple-element.197), channel_id=1, source_target_pairs={{0,8},{8,16},{16,24},{1,9},{9,17},{17,25},{2,10},{10,18},{18,26},{... | collective-permute-start | bytes 3080 | tf_op jit(solution)/shard_map/ppermute | solution.py:22
  215.3 3.8 %collective-permute-start.47 = (f32[2,1,128]{2,1,0:T(1,128)S(1)}, f32[2,1,128]{2,1,0:T(1,128)S(1)}, u32[]{:S(2)}, u32[]{:S(2)}) collective-permute-start(f32[2,1,128]{2,1,0:T(1,128)S(1)} %get-tuple-element.193), channel_id=1, source_target_pairs={{0,8},{8,16},{16,24},{1,9},{9,17},{17,25},{2,10},{10,18},{18,26},{... | collective-permute-start | bytes 3080 | tf_op jit(solution)/shard_map/ppermute | solution.py:22
  222.4 3.8 %collective-permute-start.49 = (f32[2,1,128]{2,1,0:T(1,128)S(1)}, f32[2,1,128]{2,1,0:T(1,128)S(1)}, u32[]{:S(2)}, u32[]{:S(2)}) collective-permute-start(f32[2,1,128]{2,1,0:T(1,128)S(1)} %get-tuple-element.189), channel_id=1, source_target_pairs={{0,8},{8,16},{16,24},{1,9},{9,17},{17,25},{2,10},{10,18},{18,26},{... | collective-permute-start | bytes 3080 | tf_op jit(solution)/shard_map/ppermute | solution.py:22
  229.4 3.8 %collective-permute-start.51 = (f32[2,1,128]{2,1,0:T(1,128)S(1)}, f32[2,1,128]{2,1,0:T(1,128)S(1)}, u32[]{:S(2)}, u32[]{:S(2)}) collective-permute-start(f32[2,1,128]{2,1,0:T(1,128)S(1)} %get-tuple-element.183), channel_id=1, source_target_pairs={{0,8},{8,16},{16,24},{1,9},{9,17},{17,25},{2,10},{10,18},{18,26},{... | collective-permute-start | bytes 3080 | tf_op jit(solution)/shard_map/ppermute | solution.py:22
  236.5 3.8 %collective-permute-start.53 = (f32[2,1,128]{2,1,0:T(1,128)S(1)}, f32[2,1,128]{2,1,0:T(1,128)S(1)}, u32[]{:S(2)}, u32[]{:S(2)}) collective-permute-start(f32[2,1,128]{2,1,0:T(1,128)S(1)} %get-tuple-element.181), channel_id=1, source_target_pairs={{0,8},{8,16},{16,24},{1,9},{9,17},{17,25},{2,10},{10,18},{18,26},{... | collective-permute-start | bytes 3080 | tf_op jit(solution)/shard_map/ppermute | solution.py:22
  244.0 3.8 %collective-permute-start.55 = (f32[4,1,128]{2,1,0:T(1,128)S(1)}, f32[4,1,128]{2,1,0:T(1,128)S(1)}, u32[]{:S(2)}, u32[]{:S(2)}) collective-permute-start(f32[4,1,128]{2,1,0:T(1,128)S(1)} %get-tuple-element.145), channel_id=1, source_target_pairs={{0,8},{8,16},{16,24},{1,9},{9,17},{17,25},{2,10},{10,18},{18,26},{... | collective-permute-start | bytes 6152 | tf_op jit(solution)/shard_map/ppermute | solution.py:22
  251.3 2.6 collective-permute-start.58
  256.1 2.5 collective-permute-start.59
  259.9 2.6 collective-permute-done.60
  262.6 2.6 collective-permute-start.61
  267.2 2.6 collective-permute-done.62
  271.3 2.8 collective-permute-start.63
  275.4 2.7 collective-permute-done.64
  285.6 3.0 collective-permute-start.67
  289.9 2.6 collective-permute-done.68
  292.8 3.6 %collective-permute-start.70 = (f32[8,10,1]{2,0,1:T(8,128)S(1)}, f32[8,10,1]{2,0,1:T(8,128)S(1)}, u32[]{:S(2)}, u32[]{:S(2)}) collective-permute-start(f32[8,10,1]{2,0,1:T(8,128)S(1)} %get-tuple-element.81), channel_id=1, source_target_pairs={{0,6},{1,7},{2,0},{3,1},{4,2},{5,3},{6,4},{7,5},{8,14},{9,15},{10,... | collective-permute-start | bytes 968 | tf_op jit(solution)/shard_map/ppermute | solution.py:31
  299.8 3.4 collective-permute-start.71
  307.6 3.9 %collective-permute-start.74 = (f32[16,18,1]{2,0,1:T(8,128)S(1)}, f32[16,18,1]{2,0,1:T(8,128)S(1)}, u32[]{:S(2)}, u32[]{:S(2)}) collective-permute-start(f32[16,18,1]{2,0,1:T(8,128)S(1)} %get-tuple-element.33), channel_id=1, source_target_pairs={{0,7},{1,0},{2,1},{3,2},{4,3},{5,4},{6,5},{7,6},{8,15},{9,8},{10,9... | collective-permute-start | bytes 3464 | tf_op jit(solution)/shard_map/ppermute | solution.py:31
  311.5 3.3 collective-permute-done.73
  316.8 2.9 collective-permute-start.75
  323.0 4.7 %collective-permute-start.78 = (f32[16,18,1]{2,0,1:T(8,128)S(1)}, f32[16,18,1]{2,0,1:T(8,128)S(1)}, u32[]{:S(2)}, u32[]{:S(2)}) collective-permute-start(f32[16,18,1]{2,0,1:T(8,128)S(1)} %get-tuple-element.29), channel_id=1, source_target_pairs={{0,7},{1,0},{2,1},{3,2},{4,3},{5,4},{6,5},{7,6},{8,15},{9,8},{10,9... | collective-permute-start | bytes 3464 | tf_op jit(solution)/shard_map/ppermute | solution.py:31
  327.7 3.7 %collective-permute-done.77 = f32[16,18,1]{2,0,1:T(8,128)S(1)} collective-permute-done((f32[16,18,1]{2,0,1:T(8,128)S(1)}, f32[16,18,1]{2,0,1:T(8,128)S(1)}, u32[]{:S(2)}, u32[]{:S(2)}) %collective-permute-start.77) | collective-permute-done | bytes 1184 | tf_op jit(solution)/shard_map/ppermute | solution.py:31
  333.0 2.7 collective-permute-start.79
  338.9 4.7 %collective-permute-start.82 = (f32[16,18,1]{2,0,1:T(8,128)S(1)}, f32[16,18,1]{2,0,1:T(8,128)S(1)}, u32[]{:S(2)}, u32[]{:S(2)}) collective-permute-start(f32[16,18,1]{2,0,1:T(8,128)S(1)} %get-tuple-element.25), channel_id=1, source_target_pairs={{0,7},{1,0},{2,1},{3,2},{4,3},{5,4},{6,5},{7,6},{8,15},{9,8},{10,9... | collective-permute-start | bytes 3464 | tf_op jit(solution)/shard_map/ppermute | solution.py:31
  343.7 3.8 %collective-permute-done.81 = f32[16,18,1]{2,0,1:T(8,128)S(1)} collective-permute-done((f32[16,18,1]{2,0,1:T(8,128)S(1)}, f32[16,18,1]{2,0,1:T(8,128)S(1)}, u32[]{:S(2)}, u32[]{:S(2)}) %collective-permute-start.81) | collective-permute-done | bytes 1184 | tf_op jit(solution)/shard_map/ppermute | solution.py:31
  (352 shorter events, 125.1 us)
Async XLA Ops:
  7.3 5.2 %collective-permute-start.1 = (f32[16,1,128]{2,0,1:T(8,128)S(1)}, f32[16,1,128]{2,0,1:T(8,128)S(1)}, u32[]{:S(2)}, u32[]{:S(2)}) collective-permute-start(f32[16,1,128]{2,0,1:T(8,128)S(1)} %bitcast.212), channel_id=1, source_target_pairs={{8,0},{16,8},{24,16},{9,1},{17,9},{25,17},{10,2},{18,10},{26,18},{... | collective-permute-start | bytes 24584 | tf_op jit(solution)/shard_map/ppermute | solution.py:23
  12.6 8.0 %collective-permute-start.2 = (f32[16,18,1]{2,0,1:T(8,128)S(1)}, f32[16,18,1]{2,0,1:T(8,128)S(1)}, u32[]{:S(2)}, u32[]{:S(2)}) collective-permute-start(f32[16,18,1]{2,0,1:T(8,128)S(1)} %get-tuple-element.44), channel_id=1, source_target_pairs={{0,1},{1,2},{2,3},{3,4},{4,5},{5,6},{6,7},{7,0},{8,9},{9,10},{10,1... | collective-permute-start | bytes 3464 | tf_op jit(solution)/shard_map/ppermute | solution.py:31
  14.2 8.7 %collective-permute-start.3 = (f32[16,18,1]{2,0,1:T(8,128)S(1)}, f32[16,18,1]{2,0,1:T(8,128)S(1)}, u32[]{:S(2)}, u32[]{:S(2)}) collective-permute-start(f32[16,18,1]{2,0,1:T(8,128)S(1)} %get-tuple-element.45), channel_id=1, source_target_pairs={{0,7},{1,0},{2,1},{3,2},{4,3},{5,4},{6,5},{7,6},{8,15},{9,8},{10,9... | collective-permute-start | bytes 3464 | tf_op jit(solution)/shard_map/ppermute | solution.py:31
  25.1 4.2 %collective-permute-start.4 = (f32[16,1,128]{2,0,1:T(8,128)S(1)}, f32[16,1,128]{2,0,1:T(8,128)S(1)}, u32[]{:S(2)}, u32[]{:S(2)}) collective-permute-start(f32[16,1,128]{2,0,1:T(8,128)S(1)} %bitcast.220), channel_id=1, source_target_pairs={{0,8},{8,16},{16,24},{1,9},{9,17},{17,25},{2,10},{10,18},{18,26},{... | collective-permute-start | bytes 24584 | tf_op jit(solution)/shard_map/ppermute | solution.py:22
  31.2 8.6 %collective-permute-start.6 = (f32[16,18,1]{2,0,1:T(8,128)S(1)}, f32[16,18,1]{2,0,1:T(8,128)S(1)}, u32[]{:S(2)}, u32[]{:S(2)}) collective-permute-start(f32[16,18,1]{2,0,1:T(8,128)S(1)} %get-tuple-element.40), channel_id=1, source_target_pairs={{0,1},{1,2},{2,3},{3,4},{4,5},{5,6},{6,7},{7,0},{8,9},{9,10},{10,1... | collective-permute-start | bytes 3464 | tf_op jit(solution)/shard_map/ppermute | solution.py:31
  31.3 9.5 %collective-permute-start.7 = (f32[16,18,1]{2,0,1:T(8,128)S(1)}, f32[16,18,1]{2,0,1:T(8,128)S(1)}, u32[]{:S(2)}, u32[]{:S(2)}) collective-permute-start(f32[16,18,1]{2,0,1:T(8,128)S(1)} %get-tuple-element.41), channel_id=1, source_target_pairs={{0,7},{1,0},{2,1},{3,2},{4,3},{5,4},{6,5},{7,6},{8,15},{9,8},{10,9... | collective-permute-start | bytes 3464 | tf_op jit(solution)/shard_map/ppermute | solution.py:31
  41.3 17.8 %collective-permute-start.8 = (f32[16,1,128]{2,0,1:T(8,128)S(1)}, f32[16,1,128]{2,0,1:T(8,128)S(1)}, u32[]{:S(2)}, u32[]{:S(2)}) collective-permute-start(f32[16,1,128]{2,0,1:T(8,128)S(1)} %bitcast.219), channel_id=1, source_target_pairs={{0,8},{8,16},{16,24},{1,9},{9,17},{17,25},{2,10},{10,18},{18,26},{... | collective-permute-start | bytes 24584 | tf_op jit(solution)/shard_map/ppermute | solution.py:22
  60.9 8.6 %collective-permute-start.10 = (f32[16,18,1]{2,0,1:T(8,128)S(1)}, f32[16,18,1]{2,0,1:T(8,128)S(1)}, u32[]{:S(2)}, u32[]{:S(2)}) collective-permute-start(f32[16,18,1]{2,0,1:T(8,128)S(1)} %get-tuple-element.36), channel_id=1, source_target_pairs={{0,1},{1,2},{2,3},{3,4},{4,5},{5,6},{6,7},{7,0},{8,9},{9,10},{10,1... | collective-permute-start | bytes 3464 | tf_op jit(solution)/shard_map/ppermute | solution.py:31
  60.9 10.0 %collective-permute-start.11 = (f32[16,18,1]{2,0,1:T(8,128)S(1)}, f32[16,18,1]{2,0,1:T(8,128)S(1)}, u32[]{:S(2)}, u32[]{:S(2)}) collective-permute-start(f32[16,18,1]{2,0,1:T(8,128)S(1)} %get-tuple-element.37), channel_id=1, source_target_pairs={{0,7},{1,0},{2,1},{3,2},{4,3},{5,4},{6,5},{7,6},{8,15},{9,8},{10,9... | collective-permute-start | bytes 3464 | tf_op jit(solution)/shard_map/ppermute | solution.py:31
  85.2 4.8 %collective-permute-start.12 = (f32[2,8,8,64]{3,2,1,0:T(8,128)S(1)}, f32[2,8,8,64]{3,2,1,0:T(8,128)S(1)}, u32[]{:S(2)}, u32[]{:S(2)}) collective-permute-start(f32[2,8,8,64]{3,2,1,0:T(8,128)S(1)} %pad_maximum_fusion.25), channel_id=1, source_target_pairs={{0,1},{1,0},{2,3},{3,2},{4,5},{5,4},{6,7},{7,6},{8,9},{9,8},{10,11... | collective-permute-start | bytes 98312 | tf_op jit(solution)/shard_map/ppermute | solution.py:35
  95.8 5.9 %collective-permute-start.15 = (f32[8,10,1]{2,0,1:T(8,128)S(1)}, f32[8,10,1]{2,0,1:T(8,128)S(1)}, u32[]{:S(2)}, u32[]{:S(2)}) collective-permute-start(f32[8,10,1]{2,0,1:T(8,128)S(1)} %get-tuple-element.94), channel_id=1, source_target_pairs={{0,2},{1,3},{2,4},{3,5},{4,6},{5,7},{6,0},{7,1},{8,10},{9,11},{10,... | collective-permute-start | bytes 968 | tf_op jit(solution)/shard_map/ppermute | solution.py:31
  97.1 4.7 %collective-permute-start.16 = (f32[8,10,1]{2,0,1:T(8,128)S(1)}, f32[8,10,1]{2,0,1:T(8,128)S(1)}, u32[]{:S(2)}, u32[]{:S(2)}) collective-permute-start(f32[8,10,1]{2,0,1:T(8,128)S(1)} %get-tuple-element.95), channel_id=1, source_target_pairs={{0,6},{1,7},{2,0},{3,1},{4,2},{5,3},{6,4},{7,5},{8,14},{9,15},{10,... | collective-permute-start | bytes 968 | tf_op jit(solution)/shard_map/ppermute | solution.py:31
  102.9 8.1 %collective-permute-start.17 = (f32[8,1,128]{2,1,0:T(1,128)S(1)}, f32[8,1,128]{2,1,0:T(1,128)S(1)}, u32[]{:S(2)}, u32[]{:S(2)}) collective-permute-start(f32[8,1,128]{2,1,0:T(1,128)S(1)} %get-tuple-element.110), channel_id=1, source_target_pairs={{0,8},{8,16},{16,24},{1,9},{9,17},{17,25},{2,10},{10,18},{18,26},{... | collective-permute-start | bytes 12296 | tf_op jit(solution)/shard_map/ppermute | solution.py:22
  105.8 5.2 %collective-permute-start.18 = (f32[8,1,128]{2,1,0:T(1,128)S(1)}, f32[8,1,128]{2,1,0:T(1,128)S(1)}, u32[]{:S(2)}, u32[]{:S(2)}) collective-permute-start(f32[8,1,128]{2,1,0:T(1,128)S(1)} %get-tuple-element.111), channel_id=1, source_target_pairs={{8,0},{16,8},{24,16},{9,1},{17,9},{25,17},{10,2},{18,10},{26,18},{... | collective-permute-start | bytes 12296 | tf_op jit(solution)/shard_map/ppermute | solution.py:23
  111.1 5.9 %collective-permute-start.19 = (f32[8,10,1]{2,0,1:T(8,128)S(1)}, f32[8,10,1]{2,0,1:T(8,128)S(1)}, u32[]{:S(2)}, u32[]{:S(2)}) collective-permute-start(f32[8,10,1]{2,0,1:T(8,128)S(1)} %get-tuple-element.92), channel_id=1, source_target_pairs={{0,2},{1,3},{2,4},{3,5},{4,6},{5,7},{6,0},{7,1},{8,10},{9,11},{10,... | collective-permute-start | bytes 968 | tf_op jit(solution)/shard_map/ppermute | solution.py:31
  111.7 5.3 %collective-permute-start.20 = (f32[8,10,1]{2,0,1:T(8,128)S(1)}, f32[8,10,1]{2,0,1:T(8,128)S(1)}, u32[]{:S(2)}, u32[]{:S(2)}) collective-permute-start(f32[8,10,1]{2,0,1:T(8,128)S(1)} %get-tuple-element.93), channel_id=1, source_target_pairs={{0,6},{1,7},{2,0},{3,1},{4,2},{5,3},{6,4},{7,5},{8,14},{9,15},{10,... | collective-permute-start | bytes 968 | tf_op jit(solution)/shard_map/ppermute | solution.py:31
  120.5 5.2 %collective-permute-start.22 = (f32[8,1,128]{2,1,0:T(1,128)S(1)}, f32[8,1,128]{2,1,0:T(1,128)S(1)}, u32[]{:S(2)}, u32[]{:S(2)}) collective-permute-start(f32[8,1,128]{2,1,0:T(1,128)S(1)} %get-tuple-element.107), channel_id=1, source_target_pairs={{8,0},{16,8},{24,16},{9,1},{17,9},{25,17},{10,2},{18,10},{26,18},{... | collective-permute-start | bytes 12296 | tf_op jit(solution)/shard_map/ppermute | solution.py:23
  125.7 5.8 %collective-permute-start.23 = (f32[8,10,1]{2,0,1:T(8,128)S(1)}, f32[8,10,1]{2,0,1:T(8,128)S(1)}, u32[]{:S(2)}, u32[]{:S(2)}) collective-permute-start(f32[8,10,1]{2,0,1:T(8,128)S(1)} %get-tuple-element.88), channel_id=1, source_target_pairs={{0,2},{1,3},{2,4},{3,5},{4,6},{5,7},{6,0},{7,1},{8,10},{9,11},{10,... | collective-permute-start | bytes 968 | tf_op jit(solution)/shard_map/ppermute | solution.py:31
  126.8 4.7 %collective-permute-start.24 = (f32[8,10,1]{2,0,1:T(8,128)S(1)}, f32[8,10,1]{2,0,1:T(8,128)S(1)}, u32[]{:S(2)}, u32[]{:S(2)}) collective-permute-start(f32[8,10,1]{2,0,1:T(8,128)S(1)} %get-tuple-element.89), channel_id=1, source_target_pairs={{0,6},{1,7},{2,0},{3,1},{4,2},{5,3},{6,4},{7,5},{8,14},{9,15},{10,... | collective-permute-start | bytes 968 | tf_op jit(solution)/shard_map/ppermute | solution.py:31
  136.4 3.8 %collective-permute-start.25 = (f32[2,4,4,64]{3,2,1,0:T(4,128)S(1)}, f32[2,4,4,64]{3,2,1,0:T(4,128)S(1)}, u32[]{:S(2)}, u32[]{:S(2)}) collective-permute-start(f32[2,4,4,64]{3,2,1,0:T(4,128)S(1)} %pad_maximum_fusion.65), channel_id=1, source_target_pairs={{0,2},{1,3},{2,0},{3,1},{4,6},{5,7},{6,4},{7,5},{8,10},{9,11},{10,... | collective-permute-start | bytes 24584 | tf_op jit(solution)/shard_map/ppermute | solution.py:35
  140.3 4.4 %collective-permute-start.26 = (f32[4,1,128]{2,1,0:T(1,128)S(1)}, f32[4,1,128]{2,1,0:T(1,128)S(1)}, u32[]{:S(2)}, u32[]{:S(2)}) collective-permute-start(f32[4,1,128]{2,1,0:T(1,128)S(1)} %get-tuple-element.159), channel_id=1, source_target_pairs={{0,8},{8,16},{16,24},{1,9},{9,17},{17,25},{2,10},{10,18},{18,26},{... | collective-permute-start | bytes 6152 | tf_op jit(solution)/shard_map/ppermute | solution.py:22
  142.7 4.4 %collective-permute-start.27 = (f32[4,1,128]{2,1,0:T(1,128)S(1)}, f32[4,1,128]{2,1,0:T(1,128)S(1)}, u32[]{:S(2)}, u32[]{:S(2)}) collective-permute-start(f32[4,1,128]{2,1,0:T(1,128)S(1)} %get-tuple-element.160), channel_id=1, source_target_pairs={{8,0},{16,8},{24,16},{9,1},{17,9},{25,17},{10,2},{18,10},{26,18},{... | collective-permute-start | bytes 6152 | tf_op jit(solution)/shard_map/ppermute | solution.py:23
  147.3 4.6 %collective-permute-start.28 = (f32[4,6,1]{2,0,1:T(4,128)S(1)}, f32[4,6,1]{2,0,1:T(4,128)S(1)}, u32[]{:S(2)}, u32[]{:S(2)}) collective-permute-start(f32[4,6,1]{2,0,1:T(4,128)S(1)} %get-tuple-element.139), channel_id=1, source_target_pairs={{0,4},{1,5},{2,6},{3,7},{4,0},{5,1},{6,2},{7,3},{8,12},{9,13},{10,... | collective-permute-start | bytes 296 | tf_op jit(solution)/shard_map/ppermute | solution.py:31
  149.9 4.6 %collective-permute-start.29 = (f32[4,6,1]{2,0,1:T(4,128)S(1)}, f32[4,6,1]{2,0,1:T(4,128)S(1)}, u32[]{:S(2)}, u32[]{:S(2)}) collective-permute-start(f32[4,6,1]{2,0,1:T(4,128)S(1)} %get-tuple-element.140), channel_id=1, source_target_pairs={{0,4},{1,5},{2,6},{3,7},{4,0},{5,1},{6,2},{7,3},{8,12},{9,13},{10,... | collective-permute-start | bytes 296 | tf_op jit(solution)/shard_map/ppermute | solution.py:31
  154.8 4.2 %collective-permute-start.30 = (f32[4,1,128]{2,1,0:T(1,128)S(1)}, f32[4,1,128]{2,1,0:T(1,128)S(1)}, u32[]{:S(2)}, u32[]{:S(2)}) collective-permute-start(f32[4,1,128]{2,1,0:T(1,128)S(1)} %get-tuple-element.155), channel_id=1, source_target_pairs={{0,8},{8,16},{16,24},{1,9},{9,17},{17,25},{2,10},{10,18},{18,26},{... | collective-permute-start | bytes 6152 | tf_op jit(solution)/shard_map/ppermute | solution.py:22
  157.7 4.0 %collective-permute-start.31 = (f32[4,1,128]{2,1,0:T(1,128)S(1)}, f32[4,1,128]{2,1,0:T(1,128)S(1)}, u32[]{:S(2)}, u32[]{:S(2)}) collective-permute-start(f32[4,1,128]{2,1,0:T(1,128)S(1)} %get-tuple-element.156), channel_id=1, source_target_pairs={{8,0},{16,8},{24,16},{9,1},{17,9},{25,17},{10,2},{18,10},{26,18},{... | collective-permute-start | bytes 6152 | tf_op jit(solution)/shard_map/ppermute | solution.py:23
  161.8 4.6 %collective-permute-start.32 = (f32[4,6,1]{2,0,1:T(4,128)S(1)}, f32[4,6,1]{2,0,1:T(4,128)S(1)}, u32[]{:S(2)}, u32[]{:S(2)}) collective-permute-start(f32[4,6,1]{2,0,1:T(4,128)S(1)} %get-tuple-element.135), channel_id=1, source_target_pairs={{0,4},{1,5},{2,6},{3,7},{4,0},{5,1},{6,2},{7,3},{8,12},{9,13},{10,... | collective-permute-start | bytes 296 | tf_op jit(solution)/shard_map/ppermute | solution.py:31
  162.1 4.6 %collective-permute-start.33 = (f32[4,6,1]{2,0,1:T(4,128)S(1)}, f32[4,6,1]{2,0,1:T(4,128)S(1)}, u32[]{:S(2)}, u32[]{:S(2)}) collective-permute-start(f32[4,6,1]{2,0,1:T(4,128)S(1)} %get-tuple-element.136), channel_id=1, source_target_pairs={{0,4},{1,5},{2,6},{3,7},{4,0},{5,1},{6,2},{7,3},{8,12},{9,13},{10,... | collective-permute-start | bytes 296 | tf_op jit(solution)/shard_map/ppermute | solution.py:31
  166.9 4.5 %collective-permute-start.34 = (f32[4,1,128]{2,1,0:T(1,128)S(1)}, f32[4,1,128]{2,1,0:T(1,128)S(1)}, u32[]{:S(2)}, u32[]{:S(2)}) collective-permute-start(f32[4,1,128]{2,1,0:T(1,128)S(1)} %get-tuple-element.151), channel_id=1, source_target_pairs={{0,8},{8,16},{16,24},{1,9},{9,17},{17,25},{2,10},{10,18},{18,26},{... | collective-permute-start | bytes 6152 | tf_op jit(solution)/shard_map/ppermute | solution.py:22
  173.8 4.6 %collective-permute-start.36 = (f32[4,6,1]{2,0,1:T(4,128)S(1)}, f32[4,6,1]{2,0,1:T(4,128)S(1)}, u32[]{:S(2)}, u32[]{:S(2)}) collective-permute-start(f32[4,6,1]{2,0,1:T(4,128)S(1)} %get-tuple-element.131), channel_id=1, source_target_pairs={{0,4},{1,5},{2,6},{3,7},{4,0},{5,1},{6,2},{7,3},{8,12},{9,13},{10,... | collective-permute-start | bytes 296 | tf_op jit(solution)/shard_map/ppermute | solution.py:31
  176.4 4.6 %collective-permute-start.37 = (f32[4,6,1]{2,0,1:T(4,128)S(1)}, f32[4,6,1]{2,0,1:T(4,128)S(1)}, u32[]{:S(2)}, u32[]{:S(2)}) collective-permute-start(f32[4,6,1]{2,0,1:T(4,128)S(1)} %get-tuple-element.132), channel_id=1, source_target_pairs={{0,4},{1,5},{2,6},{3,7},{4,0},{5,1},{6,2},{7,3},{8,12},{9,13},{10,... | collective-permute-start | bytes 296 | tf_op jit(solution)/shard_map/ppermute | solution.py:31
  181.8 4.6 %collective-permute-start.38 = (f32[2,2,2,64]{3,2,1,0:T(2,128)S(1)}, f32[2,2,2,64]{3,2,1,0:T(2,128)S(1)}, u32[]{:S(2)}, u32[]{:S(2)}) collective-permute-start(f32[2,2,2,64]{3,2,1,0:T(2,128)S(1)} %pad_maximum_fusion.105), channel_id=1, source_target_pairs={{0,4},{1,5},{2,6},{3,7},{4,0},{5,1},{6,2},{7,3},{8,12},{9,13},{10,... | collective-permute-start | bytes 6152 | tf_op jit(solution)/shard_map/ppermute | solution.py:35
  188.2 5.2 %collective-permute-start.40 = (f32[2,1,128]{2,1,0:T(1,128)S(1)}, f32[2,1,128]{2,1,0:T(1,128)S(1)}, u32[]{:S(2)}, u32[]{:S(2)}) collective-permute-start(f32[2,1,128]{2,1,0:T(1,128)S(1)} %get-tuple-element.210), channel_id=1, source_target_pairs={{8,0},{16,8},{24,16},{9,1},{17,9},{25,17},{10,2},{18,10},{26,18},{... | collective-permute-start | bytes 3080 | tf_op jit(solution)/shard_map/ppermute | solution.py:23
  193.7 5.6 %collective-permute-start.41 = (f32[2,1,128]{2,1,0:T(1,128)S(1)}, f32[2,1,128]{2,1,0:T(1,128)S(1)}, u32[]{:S(2)}, u32[]{:S(2)}) collective-permute-start(f32[2,1,128]{2,1,0:T(1,128)S(1)} %get-tuple-element.205), channel_id=1, source_target_pairs={{0,8},{8,16},{16,24},{1,9},{9,17},{17,25},{2,10},{10,18},{18,26},{... | collective-permute-start | bytes 3080 | tf_op jit(solution)/shard_map/ppermute | solution.py:22
  201.2 5.1 %collective-permute-start.43 = (f32[2,1,128]{2,1,0:T(1,128)S(1)}, f32[2,1,128]{2,1,0:T(1,128)S(1)}, u32[]{:S(2)}, u32[]{:S(2)}) collective-permute-start(f32[2,1,128]{2,1,0:T(1,128)S(1)} %get-tuple-element.201), channel_id=1, source_target_pairs={{0,8},{8,16},{16,24},{1,9},{9,17},{17,25},{2,10},{10,18},{18,26},{... | collective-permute-start | bytes 3080 | tf_op jit(solution)/shard_map/ppermute | solution.py:22
  208.3 5.1 %collective-permute-start.45 = (f32[2,1,128]{2,1,0:T(1,128)S(1)}, f32[2,1,128]{2,1,0:T(1,128)S(1)}, u32[]{:S(2)}, u32[]{:S(2)}) collective-permute-start(f32[2,1,128]{2,1,0:T(1,128)S(1)} %get-tuple-element.197), channel_id=1, source_target_pairs={{0,8},{8,16},{16,24},{1,9},{9,17},{17,25},{2,10},{10,18},{18,26},{... | collective-permute-start | bytes 3080 | tf_op jit(solution)/shard_map/ppermute | solution.py:22
  215.3 5.1 %collective-permute-start.47 = (f32[2,1,128]{2,1,0:T(1,128)S(1)}, f32[2,1,128]{2,1,0:T(1,128)S(1)}, u32[]{:S(2)}, u32[]{:S(2)}) collective-permute-start(f32[2,1,128]{2,1,0:T(1,128)S(1)} %get-tuple-element.193), channel_id=1, source_target_pairs={{0,8},{8,16},{16,24},{1,9},{9,17},{17,25},{2,10},{10,18},{18,26},{... | collective-permute-start | bytes 3080 | tf_op jit(solution)/shard_map/ppermute | solution.py:22
  222.4 5.1 %collective-permute-start.49 = (f32[2,1,128]{2,1,0:T(1,128)S(1)}, f32[2,1,128]{2,1,0:T(1,128)S(1)}, u32[]{:S(2)}, u32[]{:S(2)}) collective-permute-start(f32[2,1,128]{2,1,0:T(1,128)S(1)} %get-tuple-element.189), channel_id=1, source_target_pairs={{0,8},{8,16},{16,24},{1,9},{9,17},{17,25},{2,10},{10,18},{18,26},{... | collective-permute-start | bytes 3080 | tf_op jit(solution)/shard_map/ppermute | solution.py:22
  229.4 5.1 %collective-permute-start.51 = (f32[2,1,128]{2,1,0:T(1,128)S(1)}, f32[2,1,128]{2,1,0:T(1,128)S(1)}, u32[]{:S(2)}, u32[]{:S(2)}) collective-permute-start(f32[2,1,128]{2,1,0:T(1,128)S(1)} %get-tuple-element.183), channel_id=1, source_target_pairs={{0,8},{8,16},{16,24},{1,9},{9,17},{17,25},{2,10},{10,18},{18,26},{... | collective-permute-start | bytes 3080 | tf_op jit(solution)/shard_map/ppermute | solution.py:22
  236.5 5.1 %collective-permute-start.53 = (f32[2,1,128]{2,1,0:T(1,128)S(1)}, f32[2,1,128]{2,1,0:T(1,128)S(1)}, u32[]{:S(2)}, u32[]{:S(2)}) collective-permute-start(f32[2,1,128]{2,1,0:T(1,128)S(1)} %get-tuple-element.181), channel_id=1, source_target_pairs={{0,8},{8,16},{16,24},{1,9},{9,17},{17,25},{2,10},{10,18},{18,26},{... | collective-permute-start | bytes 3080 | tf_op jit(solution)/shard_map/ppermute | solution.py:22
  244.0 5.1 %collective-permute-start.55 = (f32[4,1,128]{2,1,0:T(1,128)S(1)}, f32[4,1,128]{2,1,0:T(1,128)S(1)}, u32[]{:S(2)}, u32[]{:S(2)}) collective-permute-start(f32[4,1,128]{2,1,0:T(1,128)S(1)} %get-tuple-element.145), channel_id=1, source_target_pairs={{0,8},{8,16},{16,24},{1,9},{9,17},{17,25},{2,10},{10,18},{18,26},{... | collective-permute-start | bytes 6152 | tf_op jit(solution)/shard_map/ppermute | solution.py:22
  250.9 4.6 %collective-permute-start.57 = (f32[4,6,1]{2,0,1:T(4,128)S(1)}, f32[4,6,1]{2,0,1:T(4,128)S(1)}, u32[]{:S(2)}, u32[]{:S(2)}) collective-permute-start(f32[4,6,1]{2,0,1:T(4,128)S(1)} %get-tuple-element.127), channel_id=1, source_target_pairs={{0,4},{1,5},{2,6},{3,7},{4,0},{5,1},{6,2},{7,3},{8,12},{9,13},{10,... | collective-permute-start | bytes 296 | tf_op jit(solution)/shard_map/ppermute | solution.py:31
  251.3 4.6 %collective-permute-start.58 = (f32[4,6,1]{2,0,1:T(4,128)S(1)}, f32[4,6,1]{2,0,1:T(4,128)S(1)}, u32[]{:S(2)}, u32[]{:S(2)}) collective-permute-start(f32[4,6,1]{2,0,1:T(4,128)S(1)} %get-tuple-element.128), channel_id=1, source_target_pairs={{0,4},{1,5},{2,6},{3,7},{4,0},{5,1},{6,2},{7,3},{8,12},{9,13},{10,... | collective-permute-start | bytes 296 | tf_op jit(solution)/shard_map/ppermute | solution.py:31
  256.1 3.8 %collective-permute-start.59 = (f32[4,1,128]{2,1,0:T(1,128)S(1)}, f32[4,1,128]{2,1,0:T(1,128)S(1)}, u32[]{:S(2)}, u32[]{:S(2)}) collective-permute-start(f32[4,1,128]{2,1,0:T(1,128)S(1)} %get-tuple-element.143), channel_id=1, source_target_pairs={{0,8},{8,16},{16,24},{1,9},{9,17},{17,25},{2,10},{10,18},{18,26},{... | collective-permute-start | bytes 6152 | tf_op jit(solution)/shard_map/ppermute | solution.py:22
  258.5 3.9 %collective-permute-start.60 = (f32[4,1,128]{2,1,0:T(1,128)S(1)}, f32[4,1,128]{2,1,0:T(1,128)S(1)}, u32[]{:S(2)}, u32[]{:S(2)}) collective-permute-start(f32[4,1,128]{2,1,0:T(1,128)S(1)} %get-tuple-element.144), channel_id=1, source_target_pairs={{8,0},{16,8},{24,16},{9,1},{17,9},{25,17},{10,2},{18,10},{26,18},{... | collective-permute-start | bytes 6152 | tf_op jit(solution)/shard_map/ppermute | solution.py:23
  262.6 4.6 %collective-permute-start.61 = (f32[4,6,1]{2,0,1:T(4,128)S(1)}, f32[4,6,1]{2,0,1:T(4,128)S(1)}, u32[]{:S(2)}, u32[]{:S(2)}) collective-permute-start(f32[4,6,1]{2,0,1:T(4,128)S(1)} %get-tuple-element.123), channel_id=1, source_target_pairs={{0,4},{1,5},{2,6},{3,7},{4,0},{5,1},{6,2},{7,3},{8,12},{9,13},{10,... | collective-permute-start | bytes 296 | tf_op jit(solution)/shard_map/ppermute | solution.py:31
  265.2 4.6 %collective-permute-start.62 = (f32[4,6,1]{2,0,1:T(4,128)S(1)}, f32[4,6,1]{2,0,1:T(4,128)S(1)}, u32[]{:S(2)}, u32[]{:S(2)}) collective-permute-start(f32[4,6,1]{2,0,1:T(4,128)S(1)} %get-tuple-element.124), channel_id=1, source_target_pairs={{0,4},{1,5},{2,6},{3,7},{4,0},{5,1},{6,2},{7,3},{8,12},{9,13},{10,... | collective-permute-start | bytes 296 | tf_op jit(solution)/shard_map/ppermute | solution.py:31
  271.3 4.2 %collective-permute-start.63 = (f32[8,1,128]{2,1,0:T(1,128)S(1)}, f32[8,1,128]{2,1,0:T(1,128)S(1)}, u32[]{:S(2)}, u32[]{:S(2)}) collective-permute-start(f32[8,1,128]{2,1,0:T(1,128)S(1)} %get-tuple-element.100), channel_id=1, source_target_pairs={{0,8},{8,16},{16,24},{1,9},{9,17},{17,25},{2,10},{10,18},{18,26},{... | collective-permute-start | bytes 12296 | tf_op jit(solution)/shard_map/ppermute | solution.py:22
  274.1 4.0 %collective-permute-start.64 = (f32[8,1,128]{2,1,0:T(1,128)S(1)}, f32[8,1,128]{2,1,0:T(1,128)S(1)}, u32[]{:S(2)}, u32[]{:S(2)}) collective-permute-start(f32[8,1,128]{2,1,0:T(1,128)S(1)} %get-tuple-element.101), channel_id=1, source_target_pairs={{8,0},{16,8},{24,16},{9,1},{17,9},{25,17},{10,2},{18,10},{26,18},{... | collective-permute-start | bytes 12296 | tf_op jit(solution)/shard_map/ppermute | solution.py:23
  278.2 5.9 %collective-permute-start.65 = (f32[8,10,1]{2,0,1:T(8,128)S(1)}, f32[8,10,1]{2,0,1:T(8,128)S(1)}, u32[]{:S(2)}, u32[]{:S(2)}) collective-permute-start(f32[8,10,1]{2,0,1:T(8,128)S(1)} %get-tuple-element.84), channel_id=1, source_target_pairs={{0,2},{1,3},{2,4},{3,5},{4,6},{5,7},{6,0},{7,1},{8,10},{9,11},{10,... | collective-permute-start | bytes 968 | tf_op jit(solution)/shard_map/ppermute | solution.py:31
  280.2 4.3 %collective-permute-start.66 = (f32[8,10,1]{2,0,1:T(8,128)S(1)}, f32[8,10,1]{2,0,1:T(8,128)S(1)}, u32[]{:S(2)}, u32[]{:S(2)}) collective-permute-start(f32[8,10,1]{2,0,1:T(8,128)S(1)} %get-tuple-element.85), channel_id=1, source_target_pairs={{0,6},{1,7},{2,0},{3,1},{4,2},{5,3},{6,4},{7,5},{8,14},{9,15},{10,... | collective-permute-start | bytes 968 | tf_op jit(solution)/shard_map/ppermute | solution.py:31
  285.6 4.3 %collective-permute-start.67 = (f32[8,1,128]{2,1,0:T(1,128)S(1)}, f32[8,1,128]{2,1,0:T(1,128)S(1)}, u32[]{:S(2)}, u32[]{:S(2)}) collective-permute-start(f32[8,1,128]{2,1,0:T(1,128)S(1)} %get-tuple-element.98), channel_id=1, source_target_pairs={{0,8},{8,16},{16,24},{1,9},{9,17},{17,25},{2,10},{10,18},{18,26},{... | collective-permute-start | bytes 12296 | tf_op jit(solution)/shard_map/ppermute | solution.py:22
  288.6 3.9 %collective-permute-start.68 = (f32[8,1,128]{2,1,0:T(1,128)S(1)}, f32[8,1,128]{2,1,0:T(1,128)S(1)}, u32[]{:S(2)}, u32[]{:S(2)}) collective-permute-start(f32[8,1,128]{2,1,0:T(1,128)S(1)} %get-tuple-element.99), channel_id=1, source_target_pairs={{8,0},{16,8},{24,16},{9,1},{17,9},{25,17},{10,2},{18,10},{26,18},{... | collective-permute-start | bytes 12296 | tf_op jit(solution)/shard_map/ppermute | solution.py:23
  292.6 5.9 %collective-permute-start.69 = (f32[8,10,1]{2,0,1:T(8,128)S(1)}, f32[8,10,1]{2,0,1:T(8,128)S(1)}, u32[]{:S(2)}, u32[]{:S(2)}) collective-permute-start(f32[8,10,1]{2,0,1:T(8,128)S(1)} %get-tuple-element.80), channel_id=1, source_target_pairs={{0,2},{1,3},{2,4},{3,5},{4,6},{5,7},{6,0},{7,1},{8,10},{9,11},{10,... | collective-permute-start | bytes 968 | tf_op jit(solution)/shard_map/ppermute | solution.py:31
  292.8 5.7 %collective-permute-start.70 = (f32[8,10,1]{2,0,1:T(8,128)S(1)}, f32[8,10,1]{2,0,1:T(8,128)S(1)}, u32[]{:S(2)}, u32[]{:S(2)}) collective-permute-start(f32[8,10,1]{2,0,1:T(8,128)S(1)} %get-tuple-element.81), channel_id=1, source_target_pairs={{0,6},{1,7},{2,0},{3,1},{4,2},{5,3},{6,4},{7,5},{8,14},{9,15},{10,... | collective-permute-start | bytes 968 | tf_op jit(solution)/shard_map/ppermute | solution.py:31
  299.8 4.7 %collective-permute-start.71 = (f32[16,1,128]{2,0,1:T(8,128)S(1)}, f32[16,1,128]{2,0,1:T(8,128)S(1)}, u32[]{:S(2)}, u32[]{:S(2)}) collective-permute-start(f32[16,1,128]{2,0,1:T(8,128)S(1)} %bitcast.221), channel_id=1, source_target_pairs={{0,8},{8,16},{16,24},{1,9},{9,17},{17,25},{2,10},{10,18},{18,26},{... | collective-permute-start | bytes 24584 | tf_op jit(solution)/shard_map/ppermute | solution.py:22
  306.7 8.1 %collective-permute-start.73 = (f32[16,18,1]{2,0,1:T(8,128)S(1)}, f32[16,18,1]{2,0,1:T(8,128)S(1)}, u32[]{:S(2)}, u32[]{:S(2)}) collective-permute-start(f32[16,18,1]{2,0,1:T(8,128)S(1)} %get-tuple-element.32), channel_id=1, source_target_pairs={{0,1},{1,2},{2,3},{3,4},{4,5},{5,6},{6,7},{7,0},{8,9},{9,10},{10,1... | collective-permute-start | bytes 3464 | tf_op jit(solution)/shard_map/ppermute | solution.py:31
  307.6 8.7 %collective-permute-start.74 = (f32[16,18,1]{2,0,1:T(8,128)S(1)}, f32[16,18,1]{2,0,1:T(8,128)S(1)}, u32[]{:S(2)}, u32[]{:S(2)}) collective-permute-start(f32[16,18,1]{2,0,1:T(8,128)S(1)} %get-tuple-element.33), channel_id=1, source_target_pairs={{0,7},{1,0},{2,1},{3,2},{4,3},{5,4},{6,5},{7,6},{8,15},{9,8},{10,9... | collective-permute-start | bytes 3464 | tf_op jit(solution)/shard_map/ppermute | solution.py:31
  316.8 4.2 %collective-permute-start.75 = (f32[16,1,128]{2,0,1:T(8,128)S(1)}, f32[16,1,128]{2,0,1:T(8,128)S(1)}, u32[]{:S(2)}, u32[]{:S(2)}) collective-permute-start(f32[16,1,128]{2,0,1:T(8,128)S(1)} %bitcast.222), channel_id=1, source_target_pairs={{0,8},{8,16},{16,24},{1,9},{9,17},{17,25},{2,10},{10,18},{18,26},{... | collective-permute-start | bytes 24584 | tf_op jit(solution)/shard_map/ppermute | solution.py:22
  322.9 8.5 %collective-permute-start.77 = (f32[16,18,1]{2,0,1:T(8,128)S(1)}, f32[16,18,1]{2,0,1:T(8,128)S(1)}, u32[]{:S(2)}, u32[]{:S(2)}) collective-permute-start(f32[16,18,1]{2,0,1:T(8,128)S(1)} %get-tuple-element.28), channel_id=1, source_target_pairs={{0,1},{1,2},{2,3},{3,4},{4,5},{5,6},{6,7},{7,0},{8,9},{9,10},{10,1... | collective-permute-start | bytes 3464 | tf_op jit(solution)/shard_map/ppermute | solution.py:31
  323.0 9.6 %collective-permute-start.78 = (f32[16,18,1]{2,0,1:T(8,128)S(1)}, f32[16,18,1]{2,0,1:T(8,128)S(1)}, u32[]{:S(2)}, u32[]{:S(2)}) collective-permute-start(f32[16,18,1]{2,0,1:T(8,128)S(1)} %get-tuple-element.29), channel_id=1, source_target_pairs={{0,7},{1,0},{2,1},{3,2},{4,3},{5,4},{6,5},{7,6},{8,15},{9,8},{10,9... | collective-permute-start | bytes 3464 | tf_op jit(solution)/shard_map/ppermute | solution.py:31
  333.0 4.0 %collective-permute-start.79 = (f32[16,1,128]{2,0,1:T(8,128)S(1)}, f32[16,1,128]{2,0,1:T(8,128)S(1)}, u32[]{:S(2)}, u32[]{:S(2)}) collective-permute-start(f32[16,1,128]{2,0,1:T(8,128)S(1)} %bitcast.223), channel_id=1, source_target_pairs={{0,8},{8,16},{16,24},{1,9},{9,17},{17,25},{2,10},{10,18},{18,26},{... | collective-permute-start | bytes 24584 | tf_op jit(solution)/shard_map/ppermute | solution.py:22
  338.9 8.6 %collective-permute-start.81 = (f32[16,18,1]{2,0,1:T(8,128)S(1)}, f32[16,18,1]{2,0,1:T(8,128)S(1)}, u32[]{:S(2)}, u32[]{:S(2)}) collective-permute-start(f32[16,18,1]{2,0,1:T(8,128)S(1)} %get-tuple-element.24), channel_id=1, source_target_pairs={{0,1},{1,2},{2,3},{3,4},{4,5},{5,6},{6,7},{7,0},{8,9},{9,10},{10,1... | collective-permute-start | bytes 3464 | tf_op jit(solution)/shard_map/ppermute | solution.py:31
  338.9 10.0 %collective-permute-start.82 = (f32[16,18,1]{2,0,1:T(8,128)S(1)}, f32[16,18,1]{2,0,1:T(8,128)S(1)}, u32[]{:S(2)}, u32[]{:S(2)}) collective-permute-start(f32[16,18,1]{2,0,1:T(8,128)S(1)} %get-tuple-element.25), channel_id=1, source_target_pairs={{0,7},{1,0},{2,1},{3,2},{4,3},{5,4},{6,5},{7,6},{8,15},{9,8},{10,9... | collective-permute-start | bytes 3464 | tf_op jit(solution)/shard_map/ppermute | solution.py:31
  (29 other events, 651.4 us)
where the time goes:
time: 352 us; the launch traced here: 350 us
  starting transfers between devices  169 us (48%)
  waiting for transfers between devices  120 us (34%)
  local copies, waits for them, and re-layouts  33.9 us (10%)
  other arithmetic  25.2 us (7%)
    ppermute x24, starting transfers between devices, padded(): before = lax.ppermute(last, axis, up)  73.3 us
    ppermute x32, starting transfers between devices, passed_along(): return lax.ppermute(value, axis, pairs)  62.7 us
    ppermute x32, waiting for transfers between devices, passed_along(): return lax.ppermute(value, axis, pairs)  57 us
    ppermute x24, waiting for transfers between devices, padded(): after = lax.ppermute(initial, axis, down)  51.2 us
    ppermute x24, starting transfers between devices, padded(): after = lax.ppermute(initial, axis, down)  31 us
    reshape x4, local copies, waits for them, and re-layouts, coarsen(): values.reshape(height // 2, 2, length // 2, 2, width // 2, 2)  22.7 us
    ppermute x3, waiting for transfers between devices, from_partner(): lax.ppermute(shard, axis, [(i, i ^ 1 << bit) for i in range(lax.axis_size...  11.3 us
    reduce_sum x6, other arithmetic, coarsen(): jnp.mean(values.reshape(height // 2, 2, length // 2, 2, width // 2, 2), a...  8.81 us
  transfers between devices with their start and end apart: 83, of which 54 were waited for; matrix products, arithmetic and copies ran while one was open for 6% of the time, Pallas kernels for 0%

commit v1 on v0

v1 whole, which is shorter than its diff:
```python
import functools
import jax
import jax.numpy as jnp
from jax import lax
from jax.experimental import pallas as pl
from jax.experimental.pallas import tpu as pltpu
from jax.sharding import PartitionSpec as P

LEVELS = 3
PRE = 2
POST = 2
COARSE = 8
PAD = 8
LANES = 128

relax_weight = 0.8
MESH = pl.DeviceIdType.MESH


def harmonic(a, b):
    return 2.0 * a * b / (a + b)


def lane_iota(rows):
    return lax.broadcasted_iota(jnp.int32, (rows, LANES), 1)


def from_lower(tiles):
    rolled = [pltpu.roll(v, 1, 1) for v in tiles]
    if len(tiles) == 1:
        return rolled
    edge = lane_iota(tiles[0].shape[0]) == 0
    return [jnp.where(edge, rolled[t - 1], rolled[t]) for t in range(len(tiles))]


def from_upper(tiles):
    rolled = [pltpu.roll(v, LANES - 1, 1) for v in tiles]
    if len(tiles) == 1:
        return rolled
    edge = lane_iota(tiles[0].shape[0]) == LANES - 1
    n = len(tiles)
    return [jnp.where(edge, rolled[(t + 1) % n], rolled[t]) for t in range(n)]


def select_mm(values, matrix):
    high = values.astype(jnp.bfloat16)
    low = (values - high.astype(jnp.float32)).astype(jnp.bfloat16)
    return jnp.dot(high, matrix, preferred_element_type=jnp.float32) + jnp.dot(
        low, matrix, preferred_element_type=jnp.float32
    )


def as_matrix(mask):
    return jnp.where(mask, 1.0, 0.0).astype(jnp.bfloat16)


class Level:
    def __init__(self, tiles, height, rows, unroll):
        self.tiles, self.height, self.rows, self.unroll = tiles, height, rows, unroll

    def scratch(self):
        t, h, r = self.tiles, self.height, self.rows
        grown = r + 2 * PAD
        field = pltpu.VMEM((t, h, r, LANES), jnp.float32)
        return [
            pltpu.VMEM((2, t, h, grown, LANES), jnp.float32),
            pltpu.VMEM((t, h + 2, grown, LANES), jnp.float32),
            pltpu.VMEM((t, h + 2, grown, LANES), jnp.float32),
            field, field, field, field,
            pltpu.VMEM((t, h + 1, r, LANES), jnp.float32),
            field, field,
            field,
        ]

    def bind(self, refs):
        (self.cb, self.xa, self.xb, self.cl, self.cu, self.sl, self.su, self.fh,
         self.diag, self.weight, self.rem) = refs

    def loop(self, body):
        if self.unroll:
            for h in range(self.height):
                body(h)
        else:
            def step(h, carry):
                body(h)
                return carry
            lax.fori_loop(0, self.height, step, 0)

    def clear_pads(self):
        t, h, r = self.tiles, self.height, self.rows
        for x in (self.xa, self.xb):
            x[:, :, 0:PAD, :] = jnp.zeros((t, h + 2, PAD, LANES), jnp.float32)
            x[:, :, PAD + r:, :] = jnp.zeros((t, h + 2, PAD, LANES), jnp.float32)
            x[:, 0:1, PAD:PAD + r, :] = jnp.zeros((t, 1, r, LANES), jnp.float32)
            x[:, h + 1:h + 2, PAD:PAD + r, :] = jnp.zeros((t, 1, r, LANES), jnp.float32)
        self.fh[:, 0:1] = jnp.zeros((t, 1, r, LANES), jnp.float32)

    def clear_coeff_pads(self):
        t, h, r = self.tiles, self.height, self.rows
        self.cb[0, :, :, 0:PAD, :] = jnp.ones((t, h, PAD, LANES), jnp.float32)
        self.cb[0, :, :, PAD + r:, :] = jnp.ones((t, h, PAD, LANES), jnp.float32)

    def prepare(self, first_row, total_rows):
        t_n, h_n, r = self.tiles, self.height, self.rows
        place = lax.broadcasted_iota(jnp.int32, (r, LANES), 0) + first_row
        at_start = place == 0
        at_stop = place == total_rows - 1
        outside = place == total_rows
        below = place == -1

        def body(h):
            coeff = [self.cb[0, t, h, PAD:PAD + r, :] for t in range(t_n)]
            span_lower = [harmonic(a, b) for a, b in zip(from_lower(coeff), coeff)]
            span_upper = from_upper(span_lower)
            top = min(h + 1, h_n - 1) if self.unroll else jnp.minimum(h + 1, h_n - 1)
            for t in range(t_n):
                c = coeff[t]
                lower = harmonic(self.cb[0, t, h, PAD - 1:PAD - 1 + r, :], c)
                upper = harmonic(c, self.cb[0, t, h, PAD + 1:PAD + 1 + r, :])
                self.cl[t, h] = jnp.where(at_start | outside, 0.0, lower)
                self.cu[t, h] = jnp.where(at_stop | below, 0.0, upper)
                lower = jnp.where(at_start, c, lower)
                upper = jnp.where(at_stop, c, upper)
                self.sl[t, h] = span_lower[t]
                self.su[t, h] = span_upper[t]
                height_upper = harmonic(c, self.cb[0, t, top, PAD:PAD + r, :])
                height_upper = jnp.where(h < h_n - 1, height_upper, 0.0)
                self.fh[t, h + 1] = height_upper
                diagonal = (lower + upper + span_lower[t] + span_upper[t]
                            + self.fh[t, h] + height_upper)
                weight = relax_weight / diagonal
                self.diag[t, h] = diagonal
                self.weight[t, h] = weight
                self.xa[t, h + 1, PAD:PAD + r, :] = weight * self.cb[1, t, h, PAD:PAD + r, :]
        self.loop(body)

    def near(self, x, h, start, n, tiles):
        centre = [x[t, h + 1, pl.ds(PAD + start, n), :] for t in range(self.tiles)]
        lower, upper = from_lower(centre), from_upper(centre)
        rows = pl.ds(start, n)
        out = []
        for t in range(tiles):
            out.append(
                self.cl[t, h, rows, :] * x[t, h + 1, pl.ds(PAD - 1 + start, n), :]
                + self.cu[t, h, rows, :] * x[t, h + 1, pl.ds(PAD + 1 + start, n), :]
                + self.sl[t, h, rows, :] * lower[t]
                + self.su[t, h, rows, :] * upper[t]
                + self.fh[t, h, rows, :] * x[t, h, pl.ds(PAD + start, n), :]
                + self.fh[t, h + 1, rows, :] * x[t, h + 2, pl.ds(PAD + start, n), :]
                + self.cb[1, t, h, pl.ds(PAD + start, n), :]
            )
        return centre, out

    def relax(self, x, y, start, n):
        def body(h):
            centre, near = self.near(x, h, start, n, self.tiles)
            for t in range(self.tiles):
                y[t, h + 1, pl.ds(PAD + start, n), :] = (
                    (1.0 - relax_weight) * centre[t] + self.weight[t, h, pl.ds(start, n), :] * near[t]
                )
        self.loop(body)

    def remainder(self, x, start, n, tiles, store):
        def body(h):
            centre, near = self.near(x, h, start, n, tiles)
            for t in range(tiles):
                store(t, h, near[t] - self.diag[t, h, pl.ds(start, n), :] * centre[t], centre[t])
        self.loop(body)

    def keep_remainder(self, x, start, n):
        def store(t, h, value, centre):
            self.rem[t, h, pl.ds(start, n), :] = value
        self.remainder(x, start, n, self.tiles, store)


def coarsen(fine, coarse):
    half = fine.rows // 2
    key, lane = (lax.broadcasted_iota(jnp.int32, (LANES, LANES), d) for d in (0, 1))
    into = [as_matrix(lane == (key >> 1)), as_matrix(lane == 64 + (key >> 1))]
    for t in range(coarse.tiles):
        total = None
        for side in range(2):
            f = 2 * t + side
            parts = []
            for h in range(coarse.height):
                part = None
                for plane in (2 * h, 2 * h + 1):
                    for odd in range(2):
                        piece = fine.cb[0, f, plane, pl.ds(PAD + odd, half, stride=2), :]
                        part = piece if part is None else part + piece
                parts.append(part * (0.125 * 0.25))
            for h in range(coarse.height):
                part = None
                for plane in (2 * h, 2 * h + 1):
                    for odd in range(2):
                        piece = fine.rem[f, plane, pl.ds(odd, half, stride=2), :]
                        part = piece if part is None else part + piece
                parts.append(part * 0.125)
            product = select_mm(jnp.concatenate(parts, axis=0), into[side])
            total = product if total is None else total + product
        coarse.cb[:, t, :, PAD:PAD + half, :] = total.reshape(2, coarse.height, half, LANES)


def refine_add(coarse, x, fine, y, z, wide):
    half = fine.rows // 2
    key, lane = (lax.broadcasted_iota(jnp.int32, (LANES, LANES), d) for d in (0, 1))
    out_of = [as_matrix(key == (lane >> 1)), as_matrix(key == 64 + (lane >> 1))]
    for t in range(coarse.tiles):
        stacked = x[t, 1:1 + coarse.height, PAD:PAD + half, :].reshape(coarse.height * half, LANES)
        for side in range(2):
            f = 2 * t + side
            product = select_mm(stacked, out_of[side]).reshape(coarse.height, half, LANES)
            for h in range(coarse.height):
                for odd in range(2):
                    wide[h, pl.ds(odd, half, stride=2), :] = product[h]
            for h in range(coarse.height):
                rows = wide[h, 0:fine.rows, :]
                for plane in (2 * h, 2 * h + 1):
                    z[f, plane + 1, PAD:PAD + fine.rows, :] = y[f, plane + 1, PAD:PAD + fine.rows, :] + rows


def kernel(n_cast, n_span, levels, table_ref, phase_ref, source_ref, field_ref, residual_ref, *scratch):
    for i, level in enumerate(levels):
        level.bind(scratch[11 * i:11 * i + 11])
    l0, l1, l2, l3 = levels
    (edges, halos, small, packed, gathered, tall, wide0, wide2,
     send_sem, recv_sem, send_c, recv_c, send_s, recv_s) = scratch[44:]
    c, s = lax.axis_index("cast"), lax.axis_index("span")
    height, rows, _ = phase_ref.shape
    own = slice(PAD + rows, PAD + 2 * rows)

    def span_at(offset):
        return lax.rem(s + offset + n_span, n_span)

    def cast_at(offset):
        return lax.rem(c + offset + n_cast, n_cast)

    l0.clear_coeff_pads()

    def blank(block):
        at = slice(PAD + block * rows, PAD + (block + 1) * rows)
        l0.cb[0, 0, :, at, :] = jnp.ones((height, rows, LANES), jnp.float32)
        l0.cb[1, 0, :, at, :] = jnp.zeros((height, rows, LANES), jnp.float32)
        within = slice(block * rows, (block + 1) * rows)
        for side in range(2):
            halos[side, 0, :, within, :] = jnp.ones((2, rows, LANES), jnp.float32)
            halos[side, 1, :, within, :] = jnp.zeros((2, rows, LANES), jnp.float32)

    @pl.when(c == 0)
    def _():
        blank(0)

    @pl.when(c == n_cast - 1)
    def _():
        blank(2)

    barrier = pltpu.get_barrier_semaphore()

    def greet(cast, span):
        pl.semaphore_signal(barrier, inc=1, device_id=(cast, span), device_id_type=MESH)

    for d in range(1, n_cast):
        greet(cast_at(d), s)
    for d in range(1, n_span):
        greet(c, span_at(d))

    @pl.when(c > 0)
    def _():
        greet(c - 1, span_at(1))
        greet(c - 1, span_at(-1))

    @pl.when(c < n_cast - 1)
    def _():
        greet(c + 1, span_at(1))
        greet(c + 1, span_at(-1))

    phase = phase_ref[...]
    v0, v1, v2 = table_ref[0], table_ref[1], table_ref[2]
    l0.cb[0, 0, :, own, :] = 1.0 / jnp.where(phase == 0, v0, jnp.where(phase == 1, v1, v2))
    l0.cb[1, 0, :, own, :] = source_ref[...]
    group = lane_iota(rows) >> 4
    for kind in range(2):
        for part in range(2):
            planes = [l0.cb[kind, 0, 8 * part + j, own, :] for j in range(8)]
            for side in range(2):
                merged = planes[0] if side == 0 else pltpu.roll(planes[0], 16, 1)
                for j in range(1, 8):
                    shift = (16 * j + 16 * side) % LANES
                    moved = pltpu.roll(planes[j], shift, 1) if shift else planes[j]
                    merged = jnp.where(group == j, moved, merged)
                edges[side, kind, part] = merged

    has_lower = lax.div(c + n_cast - 1, n_cast)
    has_upper = lax.div(2 * n_cast - 2 - c, n_cast)
    pl.semaphore_wait(barrier, n_cast + n_span - 2 + 2 * has_lower + 2 * has_upper)

    def block_copy(dc):
        block = 1 - dc
        return pltpu.make_async_remote_copy(
            src_ref=l0.cb.at[:, 0, :, pl.ds(PAD + rows, rows), :],
            dst_ref=l0.cb.at[:, 0, :, pl.ds(PAD + block * rows, rows), :],
            send_sem=send_sem.at[6 + (dc + 1) // 2],
            recv_sem=recv_sem.at[6 + (dc + 1) // 2],
            device_id=(c + dc, s),
            device_id_type=MESH,
        )

    def edge_copy(dc, side):
        return pltpu.make_async_remote_copy(
            src_ref=edges.at[side],
            dst_ref=halos.at[side, :, :, pl.ds((1 - dc) * rows, rows), :],
            send_sem=send_sem.at[3 * side + dc + 1],
            recv_sem=recv_sem.at[3 * side + dc + 1],
            device_id=(c + dc, span_at(2 * side - 1)),
            device_id_type=MESH,
        )

    @pl.when(c < n_cast - 1)
    def _():
        block_copy(1).start()
        edge_copy(1, 0).start()
        edge_copy(1, 1).start()

    @pl.when(c > 0)
    def _():
        block_copy(-1).start()
        edge_copy(-1, 0).start()
        edge_copy(-1, 1).start()

    edge_copy(0, 0).start()
    edge_copy(0, 1).start()

    for level in levels:
        level.clear_pads()
    for level in levels[1:]:
        level.clear_coeff_pads()
    tall[...] = jnp.zeros(tall.shape, jnp.float32)

    edge_copy(0, 0).wait()
    edge_copy(0, 1).wait()

    @pl.when(c > 0)
    def _():
        block_copy(1).wait_recv()
        edge_copy(1, 0).wait_recv()
        edge_copy(1, 1).wait_recv()
        block_copy(-1).wait_send()
        edge_copy(-1, 0).wait_send()
        edge_copy(-1, 1).wait_send()

    @pl.when(c < n_cast - 1)
    def _():
        block_copy(-1).wait_recv()
        edge_copy(-1, 0).wait_recv()
        edge_copy(-1, 1).wait_recv()
        block_copy(1).wait_send()
        edge_copy(1, 0).wait_send()
        edge_copy(1, 1).wait_send()

    first_half = lane_iota(3 * rows) < 64
    for kind in range(2):
        for part in range(2):
            above, beneath = halos[0, kind, part], halos[1, kind, part]
            for j in range(8):
                a = pltpu.roll(above, (LANES - 16 * j) % LANES, 1) if j else above
                b = pltpu.roll(beneath, 112 - 16 * j, 1) if j < 7 else beneath
                l0.cb[kind, 1, 8 * part + j, PAD:PAD + 3 * rows, :] = jnp.where(first_half, a, b)

    l0.prepare(rows * c - rows, rows * n_cast)
    l0.relax(l0.xa, l0.xb, 0, 3 * rows)
    l0.keep_remainder(l0.xb, 0, 3 * rows)
    coarsen(l0, l1)
    rows1 = rows // 2
    l1.prepare(rows1 * c - rows1, rows1 * n_cast)
    l1.relax(l1.xa, l1.xb, 0, 3 * rows1)
    l1.keep_remainder(l1.xb, rows1, rows1)

    rows2 = rows1 // 2
    for h in range(l2.height):
        for k in range(2):
            part = None
            for plane in (2 * h, 2 * h + 1):
                for odd in range(2):
                    if k == 0:
                        piece = l1.rem[0, plane, pl.ds(rows1 + odd, rows2, stride=2), :]
                    else:
                        piece = l1.cb[0, 0, plane, pl.ds(PAD + rows1 + odd, rows2, stride=2), :]
                    part = piece if part is None else part + piece
            small[h, rows2 * k:rows2 * (k + 1), :] = part * (0.125 if k == 0 else 0.125 * 0.25)
    key, lane = (lax.broadcasted_iota(jnp.int32, (LANES, LANES), d) for d in (0, 1))
    product = select_mm(small[...].reshape(8 * l2.height, LANES), as_matrix((lane == (key >> 1)) & (key < 64)))
    product = product.reshape(l2.height, 8, LANES)
    merged = product[0]
    for h in range(1, l2.height):
        merged = merged + pltpu.roll(product[h], 32 * h, 1)
    packed[...] = merged
    gathered[s, c] = merged

    copies = []
    for d in range(1, n_cast):
        copies.append(pltpu.make_async_remote_copy(
            src_ref=packed, dst_ref=gathered.at[s, c], send_sem=send_c.at[d - 1], recv_sem=recv_c.at[d - 1],
            device_id=(cast_at(d), s), device_id_type=MESH))
        copies[-1].start()
    for copy in copies:
        copy.wait()
    copies = []
    for d in range(1, n_span):
        copies.append(pltpu.make_async_remote_copy(
            src_ref=gathered.at[s], dst_ref=gathered.at[s], send_sem=send_s.at[d - 1], recv_sem=recv_s.at[d - 1],
            device_id=(c, span_at(d)), device_id_type=MESH))
        copies[-1].start()
    for copy in copies:
        copy.wait()

    quarter = lane_iota(8) >> 5
    for t in range(l2.tiles):
        for cc in range(n_cast):
            blocks = [gathered[4 * t + j, cc] for j in range(4)]
            for h in range(l2.height):
                joined = None
                for j in range(4):
                    shift = (32 * (j - h)) % LANES
                    moved = pltpu.roll(blocks[j], shift, 1) if shift else blocks[j]
                    joined = moved if joined is None else jnp.where(quarter == j, moved, joined)
                at = PAD + rows2 * cc
                l2.cb[1, t, h, at:at + rows2, :] = joined[:rows2]
                l2.cb[0, t, h, at:at + rows2, :] = joined[rows2:]

    l2.prepare(0, l2.rows)
    l2.relax(l2.xa, l2.xb, 0, l2.rows)
    l2.keep_remainder(l2.xb, 0, l2.rows)
    coarsen(l2, l3)
    l3.prepare(0, l3.rows)
    x, y = l3.xa, l3.xb
    for _ in range(COARSE - 1):
        l3.relax(x, y, 0, l3.rows)
        x, y = y, x
    refine_add(l3, x, l2, l2.xb, l2.xa, wide2)
    l2.relax(l2.xa, l2.xb, 0, l2.rows)
    l2.relax(l2.xb, l2.xa, 0, l2.rows)

    period = 64 * n_span
    place = jnp.where(lane < 96, lane, lane - LANES) + 64 * s
    place = jnp.where(place < 0, place + period, jnp.where(place >= period, place - period, place)) >> 1
    product = None
    for t in range(l2.tiles):
        stacked = l2.xa[t, 1:1 + l2.height, PAD:PAD + l2.rows, :].reshape(l2.height * l2.rows, LANES)
        term = select_mm(stacked, as_matrix(key + LANES * t == place))
        product = term if product is None else product + term
    product = product.reshape(l2.height, l2.rows, LANES)
    for h in range(l2.height):
        for odd in range(2):
            tall[h, pl.ds(PAD + odd, l2.rows, stride=2), :] = product[h]
    for h in range(l2.height):
        window = tall[h, pl.ds(pl.multiple_of(8 * c, 8), 3 * rows1), :]
        for plane in (2 * h, 2 * h + 1):
            l1.xa[0, plane + 1, PAD:PAD + 3 * rows1, :] = l1.xb[0, plane + 1, PAD:PAD + 3 * rows1, :] + window
    l1.relax(l1.xa, l1.xb, 0, 3 * rows1)
    l1.relax(l1.xb, l1.xa, 0, 3 * rows1)
    refine_add(l1, l1.xa, l0, l0.xb, l0.xa, wide0)
    l0.relax(l0.xa, l0.xb, rows - 8, rows + 16)
    l0.relax(l0.xb, l0.xa, rows - 8, rows + 16)

    def finish(t, h, value, centre):
        field_ref[h] = centre
        residual_ref[h] = value

    l0.remainder(l0.xa, rows, rows, 1, finish)


def solution(mesh):
    n_cast, n_span = mesh.shape["cast"], mesh.shape["span"]

    def shards(phase, viscosity_table, pressure_source):
        height, rows, width = phase.shape
        assert (height, rows, width) == (16, 16, LANES)
        levels = [
            Level(2, 16, 3 * rows, False),
            Level(1, 8, 3 * rows // 2, False),
            Level(n_span // 4, 4, 4 * n_cast, True),
            Level(n_span // 8, 2, 2 * n_cast, True),
        ]
        scratch = []
        for level in levels:
            scratch += level.scratch()
        dma = pltpu.SemaphoreType.DMA
        scratch += [
            pltpu.VMEM((2, 2, 2, rows, LANES), jnp.float32),
            pltpu.VMEM((2, 2, 2, 3 * rows, LANES), jnp.float32),
            pltpu.VMEM((4, 8, LANES), jnp.float32),
            pltpu.VMEM((8, LANES), jnp.float32),
            pltpu.VMEM((n_span, n_cast, 8, LANES), jnp.float32),
            pltpu.VMEM((4, 8 * n_cast + 2 * PAD, LANES), jnp.float32),
            pltpu.VMEM((8, 3 * rows, LANES), jnp.float32),
            pltpu.VMEM((2, 4 * n_cast, LANES), jnp.float32),
            dma((8,)), dma((8,)),
            dma((n_cast - 1,)), dma((n_cast - 1,)),
            dma((n_span - 1,)), dma((n_span - 1,)),
        ]
        block = jax.ShapeDtypeStruct(phase.shape, jnp.float32)
        vmem = pl.BlockSpec(memory_space=pltpu.VMEM)
        return pl.pallas_call(
            functools.partial(kernel, n_cast, n_span, levels),
            out_shape=(block, block),
            in_specs=[pl.BlockSpec(memory_space=pltpu.SMEM), vmem, vmem],
            out_specs=(vmem, vmem),
            scratch_shapes=scratch,
            compiler_params=pltpu.CompilerParams(
                collective_id=0, has_side_effects=True, vmem_limit_bytes=48 * 2**20
            ),
        )(viscosity_table, phase, pressure_source)

    placed = P(None, "cast", "span")
    return jax.shard_map(
        shards, mesh=mesh, in_specs=(placed, P(), placed), out_specs=(placed, placed), check_vma=False
    )
```

time: 352 us -> 42.3 us (0.12)
  starting transfers between devices: 169 us -> 0 us
  waiting for transfers between devices: 120 us -> 0 us
  Pallas kernels: 0 us -> 37.7 us
  local copies, waits for them, and re-layouts: 33.9 us -> 3.77 us
  other arithmetic: 25.2 us -> 0 us
    ppermute x83 -> x0, starting transfers between devices: 169 us -> none  [the longest x24 73.3 us: padded(): before = lax.ppermute(last, axis, up)]
    ppermute x83 -> x0, waiting for transfers between devices: 120 us -> none  [the longest x32 57 us: passed_along(): return lax.ppermute(value, axis, pairs)]
    pallas_call x0 -> x1, Pallas kernels: none -> 37.7 us  [shards(): pl.pallas_call(functools.partial(kernel, n_cast, n_span, levels), out_sha...]
    reshape x10 -> x0, local copies, waits for them, and re-layouts: 24 us -> none  [the longest x4 22.7 us: coarsen(): values.reshape(height // 2, 2, length // 2, 2, width // 2, 2)]
    reduce_sum x6 -> x0, other arithmetic: 8.81 us -> none  [coarsen(): jnp.mean(values.reshape(height // 2, 2, length // 2, 2, width // 2, 2), a...]
    div x22 -> x0, other arithmetic: 5.02 us -> none  [the longest x1 2.84 us: shards(): coeff = 1.0 / viscosity]
    slice x72 -> x0, local copies, waits for them, and re-layouts: 4.56 us -> none  [the longest x1 1.41 us: shards(): viscosity_table[0]]
    add x19 -> x0, other arithmetic: 3.78 us -> none  [the longest x13 2.69 us: smooth(): grown = center + relax_weight * (source_wide - image) / (scale * diagonal)]
  transfers between devices with their start and end apart: 83 -> 0, of which waited for: 54 -> 0; matrix products, arithmetic and copies ran while one was open for 6% -> 0% of each run, Pallas kernels for 0% -> 0%
where the time goes in v1:
time: 42.3 us; the launch traced here: 42.1 us
  Pallas kernels  37.7 us (89%)
  local copies, waits for them, and re-layouts  3.77 us (9%)
  between operations  0.65 us (2%)
    pallas_call x1, Pallas kernels, shards(): pl.pallas_call(functools.partial(kernel, n_cast, n_span, levels), out_sha...  37.7 us
    unnamed x8, local copies, waits for them, and re-layouts  3.77 us

profile of v1, /device:TPU:0, one launch (start us, length us, event | category | flops | bytes accessed | tf_op | source)
XLA Modules:
  0.0 42.1 jit_solution(935065287238579410)
XLA Ops:
  0.6 0.0 copy-start
  0.6 0.9 %copy-done = s32[16,16,128]{2,1,0:T(8,128)S(1)} copy-done((s32[16,16,128]{2,1,0:T(8,128)S(1)}, s32[16,16,128]{2,1,0:T(8,128)}, u32[]{:S(2)}) %copy-start) | copy-done | bytes 131096
  1.5 0.0 copy-start.1
  1.5 0.9 %copy-done.1 = f32[16,16,128]{2,1,0:T(8,128)S(1)} copy-done((f32[16,16,128]{2,1,0:T(8,128)S(1)}, f32[16,16,128]{2,1,0:T(8,128)}, u32[]{:S(2)}) %copy-start.1) | copy-done | bytes 131096
  2.4 0.0 copy-start.2
  2.4 0.7 %copy-done.2 = f32[3]{0:T(128)S(1)} copy-done((f32[3]{0:T(128)S(1)}, f32[3]{0:T(128)}, u32[]{:S(2)}) %copy-start.2) | copy-done | bytes 36
  3.1 37.7 %shard_map.50 = (f32[16,16,128]{2,1,0:T(8,128)S(1)}, f32[16,16,128]{2,1,0:T(8,128)S(1)}) custom-call(f32[3]{0:T(128)S(1)} %copy-done.2, s32[16,16,128]{2,1,0:T(8,128)S(1)} %copy-done, f32[16,16,128]{2,1,0:T(8,128)S(1)} %copy-done.1), custom_call_target="tpu_custom_call" | custom-call | tf_op jit(solution)/shard_map/pallas_call | solution.py:503
  40.8 0.7 %copy.7 = f32[16,16,128]{2,1,0:T(8,128)} copy(f32[16,16,128]{2,1,0:T(8,128)S(1)} %get-tuple-element.4) | data formatting | bytes 262144
  41.5 0.7 %copy.8 = f32[16,16,128]{2,1,0:T(8,128)} copy(f32[16,16,128]{2,1,0:T(8,128)S(1)} %get-tuple-element.5) | data formatting | bytes 262144
Async XLA Ops:
  0.6 0.9 %copy-start = (s32[16,16,128]{2,1,0:T(8,128)S(1)}, s32[16,16,128]{2,1,0:T(8,128)}, u32[]{:S(2)}) copy-start(s32[16,16,128]{2,1,0:T(8,128)} %phase_ref.1) | copy-start | bytes 393220
  1.5 0.9 %copy-start.1 = (f32[16,16,128]{2,1,0:T(8,128)S(1)}, f32[16,16,128]{2,1,0:T(8,128)}, u32[]{:S(2)}) copy-start(f32[16,16,128]{2,1,0:T(8,128)} %source_ref.1) | copy-start | bytes 393220
  2.4 0.7 %copy-start.2 = (f32[3]{0:T(128)S(1)}, f32[3]{0:T(128)}, u32[]{:S(2)}) copy-start(f32[3]{0:T(128)} %table_ref.1) | copy-start | bytes 40

commit v2 on v1

v2 whole, which is shorter than its diff:
```python
import functools
import jax
import jax.numpy as jnp
from jax import lax
from jax.experimental import pallas as pl
from jax.experimental.pallas import tpu as pltpu
from jax.sharding import PartitionSpec as P

LEVELS = 3
PRE = 2
POST = 2
COARSE = 8
PAD = 8
LANES = 128

relax_weight = 0.8
MESH = pl.DeviceIdType.MESH


def harmonic(a, b):
    return 2.0 * a * b / (a + b)


def lane_iota(rows):
    return lax.broadcasted_iota(jnp.int32, (rows, LANES), 1)


def from_lower(tiles):
    rolled = [pltpu.roll(v, 1, 1) for v in tiles]
    if len(tiles) == 1:
        return rolled
    edge = lane_iota(tiles[0].shape[0]) == 0
    return [jnp.where(edge, rolled[t - 1], rolled[t]) for t in range(len(tiles))]


def from_upper(tiles):
    rolled = [pltpu.roll(v, LANES - 1, 1) for v in tiles]
    if len(tiles) == 1:
        return rolled
    edge = lane_iota(tiles[0].shape[0]) == LANES - 1
    n = len(tiles)
    return [jnp.where(edge, rolled[(t + 1) % n], rolled[t]) for t in range(n)]


def select_mm(values, matrix):
    high = values.astype(jnp.bfloat16)
    low = (values - high.astype(jnp.float32)).astype(jnp.bfloat16)
    return jnp.dot(high, matrix, preferred_element_type=jnp.float32) + jnp.dot(
        low, matrix, preferred_element_type=jnp.float32
    )


def as_matrix(mask):
    return jnp.where(mask, 1.0, 0.0).astype(jnp.bfloat16)


class Level:
    def __init__(self, tiles, height, rows, unroll):
        self.tiles, self.height, self.rows, self.unroll = tiles, height, rows, unroll

    def scratch(self):
        t, h, r = self.tiles, self.height, self.rows
        grown = r + 2 * PAD
        field = pltpu.VMEM((t, h, r, LANES), jnp.float32)
        return [
            pltpu.VMEM((2, t, h, grown, LANES), jnp.float32),
            pltpu.VMEM((t, h + 2, grown, LANES), jnp.float32),
            pltpu.VMEM((t, h + 2, grown, LANES), jnp.float32),
            pltpu.VMEM((t, h, r + PAD, LANES), jnp.float32),
            field, field,
            pltpu.VMEM((t, h + 1, r, LANES), jnp.float32),
            field, field,
            field,
        ]

    def bind(self, refs):
        (self.cb, self.xa, self.xb, self.cl, self.sl, self.su, self.fh,
         self.diag, self.weight, self.rem) = refs

    def loop(self, body):
        def step(i, carry):
            for k in range(self.unroll):
                body(i * self.unroll + k, k)
            return carry
        if self.unroll == self.height:
            step(0, 0)
        else:
            lax.fori_loop(0, self.height // self.unroll, step, 0)

    def clear_pads(self):
        t, h, r = self.tiles, self.height, self.rows
        for x in (self.xa, self.xb):
            x[:, :, 0:PAD, :] = jnp.zeros((t, h + 2, PAD, LANES), jnp.float32)
            x[:, :, PAD + r:, :] = jnp.zeros((t, h + 2, PAD, LANES), jnp.float32)
            x[:, 0:1, PAD:PAD + r, :] = jnp.zeros((t, 1, r, LANES), jnp.float32)
            x[:, h + 1:h + 2, PAD:PAD + r, :] = jnp.zeros((t, 1, r, LANES), jnp.float32)
        self.cl[:, :, r:, :] = jnp.zeros((t, h, PAD, LANES), jnp.float32)
        self.fh[:, 0:1] = jnp.zeros((t, 1, r, LANES), jnp.float32)

    def clear_coeff_pads(self):
        t, h, r = self.tiles, self.height, self.rows
        self.cb[0, :, :, 0:PAD, :] = jnp.ones((t, h, PAD, LANES), jnp.float32)
        self.cb[0, :, :, PAD + r:, :] = jnp.ones((t, h, PAD, LANES), jnp.float32)

    def prepare(self, first_row, total_rows):
        t_n, h_n, r = self.tiles, self.height, self.rows
        place = lax.broadcasted_iota(jnp.int32, (r, LANES), 0) + first_row
        at_start = place == 0
        at_stop = place == total_rows - 1
        at_wall = at_start | (place == total_rows)
        held = {}

        def body(h, k):
            coeff = [self.cb[0, t, h, PAD:PAD + r, :] for t in range(t_n)]
            span_lower = [harmonic(a, b) for a, b in zip(from_lower(coeff), coeff)]
            span_upper = from_upper(span_lower)
            top = min(h + 1, h_n - 1) if self.unroll == h_n else jnp.minimum(h + 1, h_n - 1)
            for t in range(t_n):
                c = coeff[t]
                lower = harmonic(self.cb[0, t, h, PAD - 1:PAD - 1 + r, :], c)
                lower = jnp.where(at_wall, 0.0, lower)
                self.cl[t, h, 0:r, :] = lower
                upper = self.cl[t, h, 1:1 + r, :]
                lower = jnp.where(at_start, c, lower)
                upper = jnp.where(at_stop, c, upper)
                self.sl[t, h] = span_lower[t]
                self.su[t, h] = span_upper[t]
                height_upper = harmonic(c, self.cb[0, t, top, PAD:PAD + r, :])
                height_upper = jnp.where(h < h_n - 1, height_upper, 0.0)
                height_lower = held[t] if k else self.fh[t, h]
                held[t] = height_upper
                self.fh[t, h + 1] = height_upper
                diagonal = (lower + upper + span_lower[t] + span_upper[t]
                            + height_lower + height_upper)
                self.diag[t, h] = diagonal
                self.weight[t, h] = relax_weight / diagonal
        self.loop(body)

    def begin(self):
        r = self.rows

        def body(h, k):
            for t in range(self.tiles):
                self.xa[t, h + 1, PAD:PAD + r, :] = self.weight[t, h] * self.cb[1, t, h, PAD:PAD + r, :]
        self.loop(body)

    def near(self, x, h, start, n, tiles):
        centre = [x[t, h + 1, pl.ds(PAD + start, n), :] for t in range(self.tiles)]
        lower, upper = from_lower(centre), from_upper(centre)
        rows = pl.ds(start, n)
        out = []
        for t in range(tiles):
            out.append(
                self.cl[t, h, rows, :] * x[t, h + 1, pl.ds(PAD - 1 + start, n), :]
                + self.cl[t, h, pl.ds(start + 1, n), :] * x[t, h + 1, pl.ds(PAD + 1 + start, n), :]
                + self.sl[t, h, rows, :] * lower[t]
                + self.su[t, h, rows, :] * upper[t]
                + self.fh[t, h, rows, :] * x[t, h, pl.ds(PAD + start, n), :]
                + self.fh[t, h + 1, rows, :] * x[t, h + 2, pl.ds(PAD + start, n), :]
                + self.cb[1, t, h, pl.ds(PAD + start, n), :]
            )
        return centre, out

    def relax(self, x, y, start, n):
        def body(h, k):
            centre, near = self.near(x, h, start, n, self.tiles)
            for t in range(self.tiles):
                y[t, h + 1, pl.ds(PAD + start, n), :] = (
                    (1.0 - relax_weight) * centre[t] + self.weight[t, h, pl.ds(start, n), :] * near[t]
                )
        self.loop(body)

    def remainder(self, x, start, n, tiles, store):
        def body(h, k):
            centre, near = self.near(x, h, start, n, tiles)
            for t in range(tiles):
                store(t, h, near[t] - self.diag[t, h, pl.ds(start, n), :] * centre[t], centre[t])
        self.loop(body)

    def keep_remainder(self, x, start, n):
        def store(t, h, value, centre):
            self.rem[t, h, pl.ds(start, n), :] = value
        self.remainder(x, start, n, self.tiles, store)


def children(pieces):
    total = None
    for piece in pieces:
        total = piece if total is None else total + piece
    return total


def coarsen(fine, coarse, kind):
    half = fine.rows // 2
    key, lane = (lax.broadcasted_iota(jnp.int32, (LANES, LANES), d) for d in (0, 1))
    into = [as_matrix(lane == (key >> 1)), as_matrix(lane == 64 + (key >> 1))]
    ref, first = (fine.cb.at[0], PAD) if kind == 0 else (fine.rem, 0)
    scale = 0.125 * 0.25 if kind == 0 else 0.125
    for t in range(coarse.tiles):
        total = None
        for side in range(2):
            parts = [
                children(
                    ref[2 * t + side, plane, pl.ds(first + odd, half, stride=2), :]
                    for plane in (2 * h, 2 * h + 1) for odd in range(2)
                ) * scale
                for h in range(coarse.height)
            ]
            product = select_mm(jnp.concatenate(parts, axis=0), into[side])
            total = product if total is None else total + product
        coarse.cb[kind, t, :, PAD:PAD + half, :] = total.reshape(coarse.height, half, LANES)


def refine_add(coarse, x, fine, y, z, wide):
    half = fine.rows // 2
    key, lane = (lax.broadcasted_iota(jnp.int32, (LANES, LANES), d) for d in (0, 1))
    out_of = [as_matrix(key == (lane >> 1)), as_matrix(key == 64 + (lane >> 1))]
    for t in range(coarse.tiles):
        stacked = x[t, 1:1 + coarse.height, PAD:PAD + half, :].reshape(coarse.height * half, LANES)
        for side in range(2):
            f = 2 * t + side
            product = select_mm(stacked, out_of[side]).reshape(coarse.height, half, LANES)
            for h in range(coarse.height):
                for odd in range(2):
                    wide[h, pl.ds(odd, half, stride=2), :] = product[h]
            for h in range(coarse.height):
                rows = wide[h, 0:fine.rows, :]
                for plane in (2 * h, 2 * h + 1):
                    z[f, plane + 1, PAD:PAD + fine.rows, :] = y[f, plane + 1, PAD:PAD + fine.rows, :] + rows


def kernel(n_cast, n_span, levels, table_ref, phase_hbm, source_hbm, field_ref, residual_ref, *scratch):
    for i, level in enumerate(levels):
        level.bind(scratch[10 * i:10 * i + 10])
    l0, l1, l2, l3 = levels
    (phase_ref, edges, halos, half, small, packed, gathered, tall, wide0, wide2, load_sem,
     send_sem, recv_sem, send_c, recv_c, send_s, recv_s) = scratch[40:]
    c, s = lax.axis_index("cast"), lax.axis_index("span")
    height, rows, _ = phase_ref.shape
    rows1, rows2 = rows // 2, rows // 4
    own = slice(PAD + rows, PAD + 2 * rows)
    load_phase = pltpu.make_async_copy(phase_hbm, phase_ref, load_sem.at[0])
    load_source = pltpu.make_async_copy(source_hbm, l0.cb.at[1, 0, :, own, :], load_sem.at[1])
    load_phase.start()
    load_source.start()

    def span_at(offset):
        return lax.rem(s + offset + n_span, n_span)

    def cast_at(offset):
        return lax.rem(c + offset + n_cast, n_cast)

    def blank(block):
        at = slice(PAD + block * rows, PAD + (block + 1) * rows)
        l0.cb[0, 0, :, at, :] = jnp.ones((height, rows, LANES), jnp.float32)
        l0.cb[1, 0, :, at, :] = jnp.zeros((height, rows, LANES), jnp.float32)
        within = slice(block * rows, (block + 1) * rows)
        for side in range(2):
            halos[0, side, :, within, :] = jnp.ones((2, rows, LANES), jnp.float32)
            halos[1, side, :, within, :] = jnp.zeros((2, rows, LANES), jnp.float32)

    @pl.when(c == 0)
    def _():
        blank(0)

    @pl.when(c == n_cast - 1)
    def _():
        blank(2)

    barrier = pltpu.get_barrier_semaphore()

    def greet(cast, span):
        pl.semaphore_signal(barrier, inc=1, device_id=(cast, span), device_id_type=MESH)

    for d in range(1, n_cast):
        greet(cast_at(d), s)
    for d in range(1, n_span):
        greet(c, span_at(d))

    @pl.when(c > 0)
    def _():
        greet(c - 1, span_at(1))
        greet(c - 1, span_at(-1))

    @pl.when(c < n_cast - 1)
    def _():
        greet(c + 1, span_at(1))
        greet(c + 1, span_at(-1))

    group = lane_iota(rows) >> 4

    def pack_edges(kind):
        for part in range(2):
            planes = [l0.cb[kind, 0, 8 * part + j, own, :] for j in range(8)]
            for side in range(2):
                merged = planes[0] if side == 0 else pltpu.roll(planes[0], 16, 1)
                for j in range(1, 8):
                    shift = (16 * j + 16 * side) % LANES
                    moved = pltpu.roll(planes[j], shift, 1) if shift else planes[j]
                    merged = jnp.where(group == j, moved, merged)
                edges[kind, side, part] = merged

    load_phase.wait()
    phase = phase_ref[...]
    v0, v1, v2 = table_ref[0], table_ref[1], table_ref[2]
    l0.cb[0, 0, :, own, :] = 1.0 / jnp.where(phase == 0, v0, jnp.where(phase == 1, v1, v2))
    pack_edges(0)
    load_source.wait()
    pack_edges(1)

    has_lower = lax.div(c + n_cast - 1, n_cast)
    has_upper = lax.div(2 * n_cast - 2 - c, n_cast)
    pl.semaphore_wait(barrier, n_cast + n_span - 2 + 2 * has_lower + 2 * has_upper)

    def block_copy(kind, dc):
        block = 1 - dc
        return pltpu.make_async_remote_copy(
            src_ref=l0.cb.at[kind, 0, :, pl.ds(PAD + rows, rows), :],
            dst_ref=l0.cb.at[kind, 0, :, pl.ds(PAD + block * rows, rows), :],
            send_sem=send_sem.at[kind, 6 + (dc + 1) // 2],
            recv_sem=recv_sem.at[kind, 6 + (dc + 1) // 2],
            device_id=(c + dc, s),
            device_id_type=MESH,
        )

    def edge_copy(kind, dc, side):
        return pltpu.make_async_remote_copy(
            src_ref=edges.at[kind, side],
            dst_ref=halos.at[kind, side, :, pl.ds((1 - dc) * rows, rows), :],
            send_sem=send_sem.at[kind, 3 * side + dc + 1],
            recv_sem=recv_sem.at[kind, 3 * side + dc + 1],
            device_id=(c + dc, span_at(2 * side - 1)),
            device_id_type=MESH,
        )

    def toward(kind, dc):
        return [block_copy(kind, dc), edge_copy(kind, dc, 0), edge_copy(kind, dc, 1)]

    def send_halo(kind):
        @pl.when(c < n_cast - 1)
        def _():
            for copy in toward(kind, 1):
                copy.start()

        @pl.when(c > 0)
        def _():
            for copy in toward(kind, -1):
                copy.start()

        edge_copy(kind, 0, 0).start()
        edge_copy(kind, 0, 1).start()

    first_half = lane_iota(3 * rows) < 64

    def take_halo(kind):
        edge_copy(kind, 0, 0).wait()
        edge_copy(kind, 0, 1).wait()

        @pl.when(c > 0)
        def _():
            for copy in toward(kind, 1):
                copy.wait_recv()
            for copy in toward(kind, -1):
                copy.wait_send()

        @pl.when(c < n_cast - 1)
        def _():
            for copy in toward(kind, -1):
                copy.wait_recv()
            for copy in toward(kind, 1):
                copy.wait_send()

        for part in range(2):
            above, beneath = halos[kind, 0, part], halos[kind, 1, part]
            for j in range(8):
                a = pltpu.roll(above, (LANES - 16 * j) % LANES, 1) if j else above
                b = pltpu.roll(beneath, 112 - 16 * j, 1) if j < 7 else beneath
                l0.cb[kind, 1, 8 * part + j, PAD:PAD + 3 * rows, :] = jnp.where(first_half, a, b)

    key, lane = (lax.broadcasted_iota(jnp.int32, (LANES, LANES), d) for d in (0, 1))
    narrow = as_matrix((lane == (key >> 1)) & (key < 64))
    quarter = lane_iota(rows2) >> 5

    def pack_own(kind, ref, first, scale):
        for h in range(l2.height):
            small[h] = children(
                ref[plane, pl.ds(first + odd, rows2, stride=2), :]
                for plane in (2 * h, 2 * h + 1) for odd in range(2)
            ) * scale
        product = select_mm(small[...].reshape(rows2 * l2.height, LANES), narrow)
        product = product.reshape(l2.height, rows2, LANES)
        merged = product[0]
        for h in range(1, l2.height):
            merged = merged + pltpu.roll(product[h], 32 * h, 1)
        packed[kind] = merged
        gathered[kind, s, c] = merged

    def along_cast(kind):
        return [pltpu.make_async_remote_copy(
            src_ref=packed.at[kind], dst_ref=gathered.at[kind, s, c],
            send_sem=send_c.at[kind, d - 1], recv_sem=recv_c.at[kind, d - 1],
            device_id=(cast_at(d), s), device_id_type=MESH) for d in range(1, n_cast)]

    def along_span(kind):
        return [pltpu.make_async_remote_copy(
            src_ref=gathered.at[kind, s], dst_ref=gathered.at[kind, s],
            send_sem=send_s.at[kind, d - 1], recv_sem=recv_s.at[kind, d - 1],
            device_id=(c, span_at(d)), device_id_type=MESH) for d in range(1, n_span)]

    def start(copies):
        for copy in copies:
            copy.start()

    def finished(copies):
        for copy in copies:
            copy.wait()

    def unpack(kind):
        for t in range(l2.tiles):
            for cc in range(n_cast):
                blocks = [gathered[kind, 4 * t + j, cc] for j in range(4)]
                for h in range(l2.height):
                    joined = None
                    for j in range(4):
                        shift = (32 * (j - h)) % LANES
                        moved = pltpu.roll(blocks[j], shift, 1) if shift else blocks[j]
                        joined = moved if joined is None else jnp.where(quarter == j, moved, joined)
                    at = PAD + rows2 * cc
                    l2.cb[kind, t, h, at:at + rows2, :] = joined

    send_halo(0)
    send_halo(1)
    stacked = jnp.concatenate([
        children(
            l0.cb[0, 0, plane, pl.ds(PAD + rows + odd, rows1, stride=2), :]
            for plane in (2 * h, 2 * h + 1) for odd in range(2)
        ) * (0.125 * 0.25)
        for h in range(l1.height)
    ], axis=0)
    half[...] = select_mm(stacked, as_matrix(lane == (key >> 1))).reshape(l1.height, rows1, LANES)
    pack_own(0, half, 0, 0.125 * 0.25)
    start(along_cast(0))
    for level in levels:
        level.clear_pads()
        level.clear_coeff_pads()
    tall[...] = jnp.zeros(tall.shape, jnp.float32)
    finished(along_cast(0))
    start(along_span(0))

    take_halo(0)
    l0.prepare(rows * c - rows, rows * n_cast)
    coarsen(l0, l1, 0)
    l1.prepare(rows1 * c - rows1, rows1 * n_cast)

    take_halo(1)
    l0.begin()
    l0.relax(l0.xa, l0.xb, 0, 3 * rows)
    l0.keep_remainder(l0.xb, 0, 3 * rows)
    coarsen(l0, l1, 1)
    l1.begin()
    l1.relax(l1.xa, l1.xb, 0, 3 * rows1)
    l1.keep_remainder(l1.xb, rows1, rows1)
    pack_own(1, l1.rem.at[0], rows1, 0.125)

    start(along_cast(1))
    finished(along_span(0))
    unpack(0)
    finished(along_cast(1))
    start(along_span(1))
    l2.prepare(0, l2.rows)
    coarsen(l2, l3, 0)
    l3.prepare(0, l3.rows)
    finished(along_span(1))
    unpack(1)

    l2.begin()
    l2.relax(l2.xa, l2.xb, 0, l2.rows)
    l2.keep_remainder(l2.xb, 0, l2.rows)
    coarsen(l2, l3, 1)
    l3.begin()
    x, y = l3.xa, l3.xb
    for _ in range(COARSE - 1):
        l3.relax(x, y, 0, l3.rows)
        x, y = y, x
    refine_add(l3, x, l2, l2.xb, l2.xa, wide2)
    l2.relax(l2.xa, l2.xb, 0, l2.rows)
    l2.relax(l2.xb, l2.xa, 0, l2.rows)

    period = 64 * n_span
    place = jnp.where(lane < 96, lane, lane - LANES) + 64 * s
    place = jnp.where(place < 0, place + period, jnp.where(place >= period, place - period, place)) >> 1
    product = None
    for t in range(l2.tiles):
        stacked = l2.xa[t, 1:1 + l2.height, PAD:PAD + l2.rows, :].reshape(l2.height * l2.rows, LANES)
        term = select_mm(stacked, as_matrix(key + LANES * t == place))
        product = term if product is None else product + term
    product = product.reshape(l2.height, l2.rows, LANES)
    for h in range(l2.height):
        for odd in range(2):
            tall[h, pl.ds(PAD + odd, l2.rows, stride=2), :] = product[h]
    for h in range(l2.height):
        window = tall[h, pl.ds(pl.multiple_of(8 * c, 8), 3 * rows1), :]
        for plane in (2 * h, 2 * h + 1):
            l1.xa[0, plane + 1, PAD:PAD + 3 * rows1, :] = l1.xb[0, plane + 1, PAD:PAD + 3 * rows1, :] + window
    l1.relax(l1.xa, l1.xb, 0, 3 * rows1)
    l1.relax(l1.xb, l1.xa, 0, 3 * rows1)
    refine_add(l1, l1.xa, l0, l0.xb, l0.xa, wide0)
    l0.relax(l0.xa, l0.xb, rows - 8, rows + 16)
    l0.relax(l0.xb, l0.xa, rows - 8, rows + 16)

    def finish(t, h, value, centre):
        field_ref[h] = centre
        residual_ref[h] = value

    l0.remainder(l0.xa, rows, rows, 1, finish)


def solution(mesh):
    n_cast, n_span = mesh.shape["cast"], mesh.shape["span"]

    def shards(phase, viscosity_table, pressure_source):
        height, rows, width = phase.shape
        assert (height, rows, width) == (16, 16, LANES)
        levels = [
            Level(2, 16, 3 * rows, 4),
            Level(1, 8, 3 * rows // 2, 8),
            Level(n_span // 4, 4, 4 * n_cast, 4),
            Level(n_span // 8, 2, 2 * n_cast, 2),
        ]
        scratch = []
        for level in levels:
            scratch += level.scratch()
        dma = pltpu.SemaphoreType.DMA
        scratch += [
            pltpu.VMEM(phase.shape, jnp.int32),
            pltpu.VMEM((2, 2, 2, rows, LANES), jnp.float32),
            pltpu.VMEM((2, 2, 2, 3 * rows, LANES), jnp.float32),
            pltpu.VMEM((8, 8, LANES), jnp.float32),
            pltpu.VMEM((4, 4, LANES), jnp.float32),
            pltpu.VMEM((2, 4, LANES), jnp.float32),
            pltpu.VMEM((2, n_span, n_cast, 4, LANES), jnp.float32),
            pltpu.VMEM((4, 8 * n_cast + 2 * PAD, LANES), jnp.float32),
            pltpu.VMEM((8, 3 * rows, LANES), jnp.float32),
            pltpu.VMEM((2, 4 * n_cast, LANES), jnp.float32),
            dma((2,)),
            dma((2, 8)), dma((2, 8)),
            dma((2, n_cast - 1)), dma((2, n_cast - 1)),
            dma((2, n_span - 1)), dma((2, n_span - 1)),
        ]
        block = jax.ShapeDtypeStruct(phase.shape, jnp.float32)
        vmem = pl.BlockSpec(memory_space=pltpu.VMEM)
        anywhere = pl.BlockSpec(memory_space=pl.ANY)
        return pl.pallas_call(
            functools.partial(kernel, n_cast, n_span, levels),
            out_shape=(block, block),
            in_specs=[pl.BlockSpec(memory_space=pltpu.SMEM), anywhere, anywhere],
            out_specs=(vmem, vmem),
            scratch_shapes=scratch,
            compiler_params=pltpu.CompilerParams(
                collective_id=0, has_side_effects=True, vmem_limit_bytes=48 * 2**20
            ),
        )(viscosity_table, phase, pressure_source)

    placed = P(None, "cast", "span")
    return jax.shard_map(
        shards, mesh=mesh, in_specs=(placed, P(), placed), out_specs=(placed, placed), check_vma=False
    )
```

time: 42.3 us -> 32.1 us (0.76)
  Pallas kernels: 37.7 us -> 27.5 us
    pallas_call x1, Pallas kernels: 37.7 us -> 27.5 us  [shards(): pl.pallas_call(functools.partial(kernel, n_cast, n_span, levels), out_sha...]
where the time goes in v2:
time: 32.1 us; the launch traced here: 31.9 us
  Pallas kernels  27.5 us (86%)
  local copies, waits for them, and re-layouts  3.77 us (12%)
  between operations  0.65 us (2%)
    pallas_call x1, Pallas kernels, shards(): pl.pallas_call(functools.partial(kernel, n_cast, n_span, levels), out_sha...  27.5 us
    unnamed x8, local copies, waits for them, and re-layouts  3.77 us

profile of v2, /device:TPU:0, one launch (start us, length us, event | category | flops | bytes accessed | tf_op | source)
XLA Modules:
  0.0 31.9 jit_solution(12582174374156607081)
XLA Ops:
  0.6 0.0 copy-start
  0.6 0.9 %copy-done = s32[16,16,128]{2,1,0:T(8,128)S(1)} copy-done((s32[16,16,128]{2,1,0:T(8,128)S(1)}, s32[16,16,128]{2,1,0:T(8,128)}, u32[]{:S(2)}) %copy-start) | copy-done | bytes 131096
  1.5 0.0 copy-start.1
  1.5 0.9 %copy-done.1 = f32[16,16,128]{2,1,0:T(8,128)S(1)} copy-done((f32[16,16,128]{2,1,0:T(8,128)S(1)}, f32[16,16,128]{2,1,0:T(8,128)}, u32[]{:S(2)}) %copy-start.1) | copy-done | bytes 131096
  2.4 0.0 copy-start.2
  2.4 0.7 %copy-done.2 = f32[3]{0:T(128)S(1)} copy-done((f32[3]{0:T(128)S(1)}, f32[3]{0:T(128)}, u32[]{:S(2)}) %copy-start.2) | copy-done | bytes 36
  3.1 27.5 %shard_map.50 = (f32[16,16,128]{2,1,0:T(8,128)S(1)}, f32[16,16,128]{2,1,0:T(8,128)S(1)}) custom-call(f32[3]{0:T(128)S(1)} %copy-done.2, s32[16,16,128]{2,1,0:T(8,128)S(1)} %copy-done, f32[16,16,128]{2,1,0:T(8,128)S(1)} %copy-done.1), custom_call_target="tpu_custom_call" | custom-call | tf_op jit(solution)/shard_map/pallas_call | solution.py:553
  30.6 0.7 %copy.7 = f32[16,16,128]{2,1,0:T(8,128)} copy(f32[16,16,128]{2,1,0:T(8,128)S(1)} %get-tuple-element.4) | data formatting | bytes 262144
  31.3 0.7 %copy.8 = f32[16,16,128]{2,1,0:T(8,128)} copy(f32[16,16,128]{2,1,0:T(8,128)S(1)} %get-tuple-element.5) | data formatting | bytes 262144
Async XLA Ops:
  0.6 0.9 %copy-start = (s32[16,16,128]{2,1,0:T(8,128)S(1)}, s32[16,16,128]{2,1,0:T(8,128)}, u32[]{:S(2)}) copy-start(s32[16,16,128]{2,1,0:T(8,128)} %phase_hbm.1) | copy-start | bytes 393220
  1.5 0.9 %copy-start.1 = (f32[16,16,128]{2,1,0:T(8,128)S(1)}, f32[16,16,128]{2,1,0:T(8,128)}, u32[]{:S(2)}) copy-start(f32[16,16,128]{2,1,0:T(8,128)} %source_hbm.1) | copy-start | bytes 393220
  2.4 0.7 %copy-start.2 = (f32[3]{0:T(128)S(1)}, f32[3]{0:T(128)}, u32[]{:S(2)}) copy-start(f32[3]{0:T(128)} %table_ref.1) | copy-start | bytes 40

commit v3 on v2

--- a/solution.py
+++ b/solution.py
@@ -17,8 +17,14 @@
 MESH = pl.DeviceIdType.MESH
 
 
+def inverse(a):
+    r = pl.reciprocal(a, approx=True)
+    r = r * (2.0 - a * r)
+    return r * (2.0 - a * r)
+
+
 def harmonic(a, b):
-    return 2.0 * a * b / (a + b)
+    return 2.0 * a * b * inverse(a + b)
 
 
 def lane_iota(rows):
@@ -77,10 +83,12 @@
         (self.cb, self.xa, self.xb, self.cl, self.sl, self.su, self.fh,
          self.diag, self.weight, self.rem) = refs
 
-    def loop(self, body):
+    def loop(self, body, after=None):
         def step(i, carry):
             for k in range(self.unroll):
                 body(i * self.unroll + k, k)
+            if after is not None:
+                after(i)
             return carry
         if self.unroll == self.height:
             step(0, 0)
@@ -133,7 +141,7 @@
                 diagonal = (lower + upper + span_lower[t] + span_upper[t]
                             + height_lower + height_upper)
                 self.diag[t, h] = diagonal
-                self.weight[t, h] = relax_weight / diagonal
+                self.weight[t, h] = relax_weight * inverse(diagonal)
         self.loop(body)
 
     def begin(self):
@@ -170,15 +178,47 @@
                 )
         self.loop(body)
 
-    def remainder(self, x, start, n, tiles, store):
+    def relax_held(self, sweeps):
+        t_n, h_n, r = self.tiles, self.height, self.rows
+        at = slice(PAD, PAD + r)
+        cells = [(t, h) for h in range(h_n) for t in range(t_n)]
+        weight = {k: self.weight[k[0], k[1]] for k in cells}
+        base = {k: weight[k] * self.cb[1, k[0], k[1], at, :] for k in cells}
+        cast_lower = {k: weight[k] * self.cl[k[0], k[1], 0:r, :] for k in cells}
+        cast_upper = {k: weight[k] * self.cl[k[0], k[1], 1:1 + r, :] for k in cells}
+        span_lower = {k: weight[k] * self.sl[k[0], k[1]] for k in cells}
+        span_upper = {k: weight[k] * self.su[k[0], k[1]] for k in cells}
+        height_lower = {k: weight[k] * self.fh[k[0], k[1]] for k in cells}
+        height_upper = {k: weight[k] * self.fh[k[0], k[1] + 1] for k in cells}
+        x = base
+        for _ in range(sweeps - 1):
+            new = {}
+            for h in range(h_n):
+                plane = [x[t, h] for t in range(t_n)]
+                lower, upper = from_lower(plane), from_upper(plane)
+                for t in range(t_n):
+                    k = (t, h)
+                    local = (1.0 - relax_weight) * x[k] + base[k]
+                    if h > 0:
+                        local = local + height_lower[k] * x[t, h - 1]
+                    if h < h_n - 1:
+                        local = local + height_upper[k] * x[t, h + 1]
+                    cast = (cast_lower[k] * pltpu.roll(x[k], 1, 0)
+                            + cast_upper[k] * pltpu.roll(x[k], r - 1, 0))
+                    new[k] = local + cast + (span_lower[k] * lower[t] + span_upper[k] * upper[t])
+            x = new
+        for t, h in cells:
+            self.xa[t, h + 1, at, :] = x[t, h]
+
+    def remainder(self, x, start, n, tiles, store, after=None):
         def body(h, k):
             centre, near = self.near(x, h, start, n, tiles)
             for t in range(tiles):
-                store(t, h, near[t] - self.diag[t, h, pl.ds(start, n), :] * centre[t], centre[t])
-        self.loop(body)
+                store(t, h, near[t] - self.diag[t, h, pl.ds(start, n), :] * centre[t])
+        self.loop(body, after)
 
     def keep_remainder(self, x, start, n):
-        def store(t, h, value, centre):
+        def store(t, h, value):
             self.rem[t, h, pl.ds(start, n), :] = value
         self.remainder(x, start, n, self.tiles, store)
 
@@ -211,12 +251,12 @@
         coarse.cb[kind, t, :, PAD:PAD + half, :] = total.reshape(coarse.height, half, LANES)
 
 
-def refine_add(coarse, x, fine, y, z, wide):
-    half = fine.rows // 2
+def refine_add(coarse, x, fine, y, z, wide, start, n):
+    half, first = n // 2, start // 2
     key, lane = (lax.broadcasted_iota(jnp.int32, (LANES, LANES), d) for d in (0, 1))
     out_of = [as_matrix(key == (lane >> 1)), as_matrix(key == 64 + (lane >> 1))]
     for t in range(coarse.tiles):
-        stacked = x[t, 1:1 + coarse.height, PAD:PAD + half, :].reshape(coarse.height * half, LANES)
+        stacked = x[t, 1:1 + coarse.height, PAD + first:PAD + first + half, :].reshape(coarse.height * half, LANES)
         for side in range(2):
             f = 2 * t + side
             product = select_mm(stacked, out_of[side]).reshape(coarse.height, half, LANES)
@@ -224,16 +264,17 @@
                 for odd in range(2):
                     wide[h, pl.ds(odd, half, stride=2), :] = product[h]
             for h in range(coarse.height):
-                rows = wide[h, 0:fine.rows, :]
+                rows = wide[h, 0:n, :]
                 for plane in (2 * h, 2 * h + 1):
-                    z[f, plane + 1, PAD:PAD + fine.rows, :] = y[f, plane + 1, PAD:PAD + fine.rows, :] + rows
-
-
-def kernel(n_cast, n_span, levels, table_ref, phase_hbm, source_hbm, field_ref, residual_ref, *scratch):
+                    at = pl.ds(PAD + start, n)
+                    z[f, plane + 1, at, :] = y[f, plane + 1, at, :] + rows
+
+
+def kernel(n_cast, n_span, levels, table_hbm, phase_hbm, source_hbm, field_hbm, residual_hbm, *scratch):
     for i, level in enumerate(levels):
         level.bind(scratch[10 * i:10 * i + 10])
     l0, l1, l2, l3 = levels
-    (phase_ref, edges, halos, half, small, packed, gathered, tall, wide0, wide2, load_sem,
+    (table_ref, phase_ref, edges, halos, half, small, packed, gathered, tall, wide0, wide2, load_sem, save_sem,
      send_sem, recv_sem, send_c, recv_c, send_s, recv_s) = scratch[40:]
     c, s = lax.axis_index("cast"), lax.axis_index("span")
     height, rows, _ = phase_ref.shape
@@ -241,6 +282,8 @@
     own = slice(PAD + rows, PAD + 2 * rows)
     load_phase = pltpu.make_async_copy(phase_hbm, phase_ref, load_sem.at[0])
     load_source = pltpu.make_async_copy(source_hbm, l0.cb.at[1, 0, :, own, :], load_sem.at[1])
+    load_table = pltpu.make_async_copy(table_hbm, table_ref, load_sem.at[2])
+    load_table.start()
     load_phase.start()
     load_source.start()
 
@@ -300,6 +343,7 @@
                     merged = jnp.where(group == j, moved, merged)
                 edges[kind, side, part] = merged
 
+    load_table.wait()
     load_phase.wait()
     phase = phase_ref[...]
     v0, v1, v2 = table_ref[0], table_ref[1], table_ref[2]
@@ -477,12 +521,8 @@
     l2.relax(l2.xa, l2.xb, 0, l2.rows)
     l2.keep_remainder(l2.xb, 0, l2.rows)
     coarsen(l2, l3, 1)
-    l3.begin()
-    x, y = l3.xa, l3.xb
-    for _ in range(COARSE - 1):
-        l3.relax(x, y, 0, l3.rows)
-        x, y = y, x
-    refine_add(l3, x, l2, l2.xb, l2.xa, wide2)
+    l3.relax_held(COARSE)
+    refine_add(l3, l3.xa, l2, l2.xb, l2.xa, wide2, 0, l2.rows)
     l2.relax(l2.xa, l2.xb, 0, l2.rows)
     l2.relax(l2.xb, l2.xa, 0, l2.rows)
 
@@ -504,15 +544,26 @@
             l1.xa[0, plane + 1, PAD:PAD + 3 * rows1, :] = l1.xb[0, plane + 1, PAD:PAD + 3 * rows1, :] + window
     l1.relax(l1.xa, l1.xb, 0, 3 * rows1)
     l1.relax(l1.xb, l1.xa, 0, 3 * rows1)
-    refine_add(l1, l1.xa, l0, l0.xb, l0.xa, wide0)
+    refine_add(l1, l1.xa, l0, l0.xb, l0.xa, wide0, rows - 8, rows + 16)
     l0.relax(l0.xa, l0.xb, rows - 8, rows + 16)
     l0.relax(l0.xb, l0.xa, rows - 8, rows + 16)
 
-    def finish(t, h, value, centre):
-        field_ref[h] = centre
-        residual_ref[h] = value
-
-    l0.remainder(l0.xa, rows, rows, 1, finish)
+    save_field = pltpu.make_async_copy(
+        l0.xa.at[0, pl.ds(1, height), pl.ds(PAD + rows, rows), :], field_hbm, load_sem.at[0])
+    save_field.start()
+
+    def save_group(i):
+        planes = pl.ds(i * l0.unroll, l0.unroll)
+        return pltpu.make_async_copy(
+            l0.rem.at[0, planes, pl.ds(rows, rows), :], residual_hbm.at[planes], save_sem.at[i])
+
+    def finish(t, h, value):
+        l0.rem[t, h, rows:2 * rows, :] = value
+
+    l0.remainder(l0.xa, rows, rows, 1, finish, lambda i: save_group(i).start())
+    save_field.wait()
+    for i in range(height // l0.unroll):
+        save_group(i).wait()
 
 
 def solution(mesh):
@@ -532,6 +583,7 @@
             scratch += level.scratch()
         dma = pltpu.SemaphoreType.DMA
         scratch += [
+            pltpu.SMEM((3,), jnp.float32),
             pltpu.VMEM(phase.shape, jnp.int32),
             pltpu.VMEM((2, 2, 2, rows, LANES), jnp.float32),
             pltpu.VMEM((2, 2, 2, 3 * rows, LANES), jnp.float32),
@@ -542,22 +594,21 @@
             pltpu.VMEM((4, 8 * n_cast + 2 * PAD, LANES), jnp.float32),
             pltpu.VMEM((8, 3 * rows, LANES), jnp.float32),
             pltpu.VMEM((2, 4 * n_cast, LANES), jnp.float32),
-            dma((2,)),
+            dma((3,)), dma((4,)),
             dma((2, 8)), dma((2, 8)),
             dma((2, n_cast - 1)), dma((2, n_cast - 1)),
             dma((2, n_span - 1)), dma((2, n_span - 1)),
         ]
         block = jax.ShapeDtypeStruct(phase.shape, jnp.float32)
-        vmem = pl.BlockSpec(memory_space=pltpu.VMEM)
-        anywhere = pl.BlockSpec(memory_space=pl.ANY)
+        anywhere = pl.BlockSpec(memory_space=pltpu.HBM)
         return pl.pallas_call(
             functools.partial(kernel, n_cast, n_span, levels),
             out_shape=(block, block),
-            in_specs=[pl.BlockSpec(memory_space=pltpu.SMEM), anywhere, anywhere],
-            out_specs=(vmem, vmem),
+            in_specs=[anywhere, anywhere, anywhere],
+            out_specs=(anywhere, anywhere),
             scratch_shapes=scratch,
             compiler_params=pltpu.CompilerParams(
-                collective_id=0, has_side_effects=True, vmem_limit_bytes=48 * 2**20
+                collective_id=0, has_side_effects=True, vmem_limit_bytes=63 * 2**20
             ),
         )(viscosity_table, phase, pressure_source)
 

time: 32.1 us -> 31.3 us (0.975)
  local copies, waits for them, and re-layouts: 3.77 us -> 2.26 us
  Pallas kernels: 27.5 us -> 28.3 us
    unnamed x8 -> x4, local copies, waits for them, and re-layouts: 3.77 us -> 2.26 us
    pallas_call x1, Pallas kernels: 27.5 us -> 28.3 us  [shards(): pl.pallas_call(functools.partial(kernel, n_cast, n_span, levels), out_sha...]
where the time goes in v3:
time: 31.3 us; the launch traced here: 31.2 us
  Pallas kernels  28.3 us (90%)
  local copies, waits for them, and re-layouts  2.26 us (7%)
  between operations  0.65 us (2%)
    pallas_call x1, Pallas kernels, shards(): pl.pallas_call(functools.partial(kernel, n_cast, n_span, levels), out_sha...  28.3 us
    unnamed x4, local copies, waits for them, and re-layouts  2.26 us

profile of v3, /device:TPU:0, one launch (start us, length us, event | category | flops | bytes accessed | tf_op | source)
XLA Modules:
  0.0 31.2 jit_solution(17704328917003488175)
XLA Ops:
  0.6 28.3 %shard_map.50 = (f32[16,16,128]{2,1,0:T(8,128)}, f32[16,16,128]{2,1,0:T(8,128)}) custom-call(f32[3]{0:T(128)} %table_hbm.1, s32[16,16,128]{2,1,0:T(8,128)} %phase_hbm.1, f32[16,16,128]{2,1,0:T(8,128)} %source_hbm.1), custom_call_target="tpu_custom_call" | custom-call | tf_op jit(solution)/shard_map/pallas_call | solution.py:604
  28.9 0.0 copy-start
  28.9 1.6 %copy.7 = f32[16,16,128]{2,1,0:T(8,128)} copy(f32[16,16,128]{2,1,0:T(8,128)} %get-tuple-element.4) | data formatting | bytes 262144
  30.5 0.0 copy-done
  30.5 0.7 %copy.8 = f32[16,16,128]{2,1,0:T(8,128)} copy(f32[16,16,128]{2,1,0:T(8,128)S(1)} %copy-done) | data formatting | bytes 262144
Async XLA Ops:
  28.9 1.6 %copy-start = (f32[16,16,128]{2,1,0:T(8,128)S(1)}, f32[16,16,128]{2,1,0:T(8,128)}, u32[]{:S(2)}) copy-start(f32[16,16,128]{2,1,0:T(8,128)} %get-tuple-element.5) | copy-start | bytes 393220

commit v4 on v3

--- a/solution.py
+++ b/solution.py
@@ -270,21 +270,19 @@
                     z[f, plane + 1, at, :] = y[f, plane + 1, at, :] + rows
 
 
-def kernel(n_cast, n_span, levels, table_hbm, phase_hbm, source_hbm, field_hbm, residual_hbm, *scratch):
+def kernel(n_cast, n_span, levels, coeff_ref, source_ref, field_ref, residual_ref, *scratch):
     for i, level in enumerate(levels):
         level.bind(scratch[10 * i:10 * i + 10])
     l0, l1, l2, l3 = levels
-    (table_ref, phase_ref, edges, halos, half, small, packed, gathered, tall, wide0, wide2, load_sem, save_sem,
+    (edges, halos, half, small, packed, gathered, tall, wide0, wide2, load_sem,
      send_sem, recv_sem, send_c, recv_c, send_s, recv_s) = scratch[40:]
     c, s = lax.axis_index("cast"), lax.axis_index("span")
-    height, rows, _ = phase_ref.shape
+    height, rows, _ = coeff_ref.shape
     rows1, rows2 = rows // 2, rows // 4
     own = slice(PAD + rows, PAD + 2 * rows)
-    load_phase = pltpu.make_async_copy(phase_hbm, phase_ref, load_sem.at[0])
-    load_source = pltpu.make_async_copy(source_hbm, l0.cb.at[1, 0, :, own, :], load_sem.at[1])
-    load_table = pltpu.make_async_copy(table_hbm, table_ref, load_sem.at[2])
-    load_table.start()
-    load_phase.start()
+    load_coeff = pltpu.make_async_copy(coeff_ref, l0.cb.at[0, 0, :, own, :], load_sem.at[0])
+    load_source = pltpu.make_async_copy(source_ref, l0.cb.at[1, 0, :, own, :], load_sem.at[1])
+    load_coeff.start()
     load_source.start()
 
     def span_at(offset):
@@ -343,11 +341,7 @@
                     merged = jnp.where(group == j, moved, merged)
                 edges[kind, side, part] = merged
 
-    load_table.wait()
-    load_phase.wait()
-    phase = phase_ref[...]
-    v0, v1, v2 = table_ref[0], table_ref[1], table_ref[2]
-    l0.cb[0, 0, :, own, :] = 1.0 / jnp.where(phase == 0, v0, jnp.where(phase == 1, v1, v2))
+    load_coeff.wait()
     pack_edges(0)
     load_source.wait()
     pack_edges(1)
@@ -549,21 +543,14 @@
     l0.relax(l0.xb, l0.xa, rows - 8, rows + 16)
 
     save_field = pltpu.make_async_copy(
-        l0.xa.at[0, pl.ds(1, height), pl.ds(PAD + rows, rows), :], field_hbm, load_sem.at[0])
+        l0.xa.at[0, pl.ds(1, height), pl.ds(PAD + rows, rows), :], field_ref, load_sem.at[0])
     save_field.start()
 
-    def save_group(i):
-        planes = pl.ds(i * l0.unroll, l0.unroll)
-        return pltpu.make_async_copy(
-            l0.rem.at[0, planes, pl.ds(rows, rows), :], residual_hbm.at[planes], save_sem.at[i])
-
     def finish(t, h, value):
-        l0.rem[t, h, rows:2 * rows, :] = value
-
-    l0.remainder(l0.xa, rows, rows, 1, finish, lambda i: save_group(i).start())
+        residual_ref[h] = value
+
+    l0.remainder(l0.xa, rows, rows, 1, finish)
     save_field.wait()
-    for i in range(height // l0.unroll):
-        save_group(i).wait()
 
 
 def solution(mesh):
@@ -583,8 +570,6 @@
             scratch += level.scratch()
         dma = pltpu.SemaphoreType.DMA
         scratch += [
-            pltpu.SMEM((3,), jnp.float32),
-            pltpu.VMEM(phase.shape, jnp.int32),
             pltpu.VMEM((2, 2, 2, rows, LANES), jnp.float32),
             pltpu.VMEM((2, 2, 2, 3 * rows, LANES), jnp.float32),
             pltpu.VMEM((8, 8, LANES), jnp.float32),
@@ -594,23 +579,27 @@
             pltpu.VMEM((4, 8 * n_cast + 2 * PAD, LANES), jnp.float32),
             pltpu.VMEM((8, 3 * rows, LANES), jnp.float32),
             pltpu.VMEM((2, 4 * n_cast, LANES), jnp.float32),
-            dma((3,)), dma((4,)),
+            dma((2,)),
             dma((2, 8)), dma((2, 8)),
             dma((2, n_cast - 1)), dma((2, n_cast - 1)),
             dma((2, n_span - 1)), dma((2, n_span - 1)),
         ]
+        kinds = lax.broadcasted_iota(jnp.int32, (3,) + phase.shape, 0)
+        table = (1.0 / viscosity_table)[:, None, None, None]
+        coeff = jnp.sum(jnp.where(kinds == phase[None], table, 0.0), axis=0)
         block = jax.ShapeDtypeStruct(phase.shape, jnp.float32)
-        anywhere = pl.BlockSpec(memory_space=pltpu.HBM)
+        anywhere = pl.BlockSpec(memory_space=pl.ANY)
+        vmem = pl.BlockSpec(memory_space=pltpu.VMEM)
         return pl.pallas_call(
             functools.partial(kernel, n_cast, n_span, levels),
             out_shape=(block, block),
-            in_specs=[anywhere, anywhere, anywhere],
-            out_specs=(anywhere, anywhere),
+            in_specs=[anywhere, anywhere],
+            out_specs=(vmem, vmem),
             scratch_shapes=scratch,
             compiler_params=pltpu.CompilerParams(
-                collective_id=0, has_side_effects=True, vmem_limit_bytes=63 * 2**20
+                collective_id=0, has_side_effects=True, vmem_limit_bytes=40 * 2**20
             ),
-        )(viscosity_table, phase, pressure_source)
+        )(coeff, pressure_source)
 
     placed = P(None, "cast", "span")
     return jax.shard_map(

time: 31.3 us -> 31.5 us (level)
  other arithmetic: 0 us -> 1.72 us
  local copies, waits for them, and re-layouts: 2.26 us -> 1.32 us
  Pallas kernels: 28.3 us -> 27.7 us
    reduce_sum x0 -> x1, other arithmetic: none -> 1.06 us  [shards(): coeff = jnp.sum(jnp.where(kinds == phase[None], table, 0.0), axis=0)]
    unnamed x4, local copies, waits for them, and re-layouts: 2.26 us -> 1.32 us
    div x0 -> x1, other arithmetic: none -> 0.66 us  [shards(): table = (1.0 / viscosity_table)[:, None, None, None]]
    pallas_call x1, Pallas kernels: 28.3 us -> 27.7 us  [shards(): pl.pallas_call(functools.partial(kernel, n_cast, n_span, levels), out_sha...]
where the time goes in v4:
time: 31.5 us; the launch traced here: 31.3 us
  Pallas kernels  27.7 us (88%)
  other arithmetic  1.72 us (5%)
  local copies, waits for them, and re-layouts  1.32 us (4%)
  between operations  0.65 us (2%)
    pallas_call x1, Pallas kernels, shards(): pl.pallas_call(functools.partial(kernel, n_cast, n_span, levels), out_sha...  27.7 us
    unnamed x4, local copies, waits for them, and re-layouts  1.32 us
    reduce_sum x1, other arithmetic, shards(): coeff = jnp.sum(jnp.where(kinds == phase[None], table, 0.0), axis=0)  1.06 us
    div x1, other arithmetic, shards(): table = (1.0 / viscosity_table)[:, None, None, None]  0.66 us

profile of v4, /device:TPU:0, one launch (start us, length us, event | category | flops | bytes accessed | tf_op | source)
XLA Modules:
  0.0 31.3 jit_solution(16727270725027418344)
XLA Ops:
  0.6 0.7 %broadcast_divide_fusion = f32[3]{0:T(128)S(1)} fusion(f32[3]{0:T(128)} %param.4), kind=kLoop, calls=%fused_computation.2 | loop fusion | flops 3 | bytes 24 | tf_op jit(solution)/shard_map/div | solution.py:588
  1.3 0.0 copy-start
  1.3 1.1 %select_reduce_fusion.coeff_ref = f32[16,16,128]{2,1,0:T(8,128)S(1)} fusion(f32[3]{0:T(128)S(1)} %broadcast_divide_fusion, s32[16,16,128]{2,1,0:T(8,128)} %param.3), kind=kLoop, calls=%fused_computation | loop fusion | flops 262144 | bytes 262156 | tf_op jit(solution)/shard_map/reduce_sum | solution.py:589
  2.4 0.0 copy-done
  2.4 27.7 %shard_map.50 = (f32[16,16,128]{2,1,0:T(8,128)S(1)}, f32[16,16,128]{2,1,0:T(8,128)S(1)}) custom-call(f32[16,16,128]{2,1,0:T(8,128)S(1)} %select_reduce_fusion.coeff_ref, f32[16,16,128]{2,1,0:T(8,128)S(1)} %copy-done), custom_call_target="tpu_custom_call" | custom-call | tf_op jit(solution)/shard_map/pallas_call | solution.py:593
  30.0 0.7 %copy.7 = f32[16,16,128]{2,1,0:T(8,128)} copy(f32[16,16,128]{2,1,0:T(8,128)S(1)} %get-tuple-element.4) | data formatting | bytes 262144
  30.7 0.7 %copy.8 = f32[16,16,128]{2,1,0:T(8,128)} copy(f32[16,16,128]{2,1,0:T(8,128)S(1)} %get-tuple-element.5) | data formatting | bytes 262144
Async XLA Ops:
  1.3 1.1 %copy-start = (f32[16,16,128]{2,1,0:T(8,128)S(1)}, f32[16,16,128]{2,1,0:T(8,128)}, u32[]{:S(2)}) copy-start(f32[16,16,128]{2,1,0:T(8,128)} %source_ref.1) | copy-start | bytes 393220
